TPU v7x, 32 devices: a whole 2x2x4 slice. The times are simulated.
32 devices in a mesh: groups: 2 (over x), dp: 16 (over z, y, core).
Axes of the slice: x: 2, y: 2, z: 4, core: 2. Of those that a mesh axis runs over, the one named last changes fastest.
Arguments:
- tokens: bfloat16 [4096, 2048], P(('groups', 'dp')), parts along dimension 0, may hold values from -6 to 6
- mask_positions: int32 [4096], P(('groups', 'dp')), parts along dimension 0, may hold values 0 or 1
- mask_embed: bfloat16 [2048], replicated, may hold values from -6 to 6
- queries: bfloat16 [4096, 2048], P(('groups', 'dp')), parts along dimension 0, may hold values from -70 to 70
- new_keys: bfloat16 [4096, 256], P(('groups', 'dp')), parts along dimension 0, may hold values from -10 to 10
- new_values: bfloat16 [4096, 256], P(('groups', 'dp')), parts along dimension 0, may hold values from -10 to 10
- cache_keys: bfloat16 [128, 1024, 256], P(('groups', 'dp')), parts along dimension 0, may hold values from -12 to 12
- cache_values: bfloat16 [128, 1024, 256], P(('groups', 'dp')), parts along dimension 0, may hold values from -10 to 10
- prefix_lengths: int32 [128], P(('groups', 'dp')), parts along dimension 0, may hold values from 2 to 1024, as said below
- expert_ids: int32 [4096, 8], P(('groups', 'dp')), parts along dimension 0, may hold values from 0 to 15, all different within a row; in each aligned block of 128 rows (0 to 127, 128 to 255, ...) at most 72 rows name the same one
- gate_probs: float32 [4096, 8], P(('groups', 'dp')), parts along dimension 0, may hold values from 0.05 to 0.5
- norm_gain: bfloat16 [2048], replicated, may hold values from 0.099609375 to 1.8984375
- gate_quant: bfloat16 [16, 2048, 512], P('dp'), may hold values from -0.125 to 0.125
- gate_scale: float32 [16, 16, 4], P('dp'), may hold values from 0.3 to 3
- up_quant: bfloat16 [16, 2048, 512], P('dp'), may hold values from -0.125 to 0.125
- up_scale: float32 [16, 16, 4], P('dp'), may hold values from 0.3 to 3
- down_quant: bfloat16 [16, 512, 2048], P('dp'), may hold values from -0.25 to 0.25
- down_scale: float32 [16, 4, 16], P('dp'), may hold values from 0.3 to 3
Outputs:
- mixed: bfloat16 [4096, 2048], P(('groups', 'dp')), parts along dimension 0
There are 2 independent parts, one for each index of `groups`. A program takes and returns all parts, laid end to end along the dimension named above; an argument that names none is the same for every part. Nothing has to cross between parts.
Inputs may be any that keep to these rules, and one draw needn't show every extreme that they name: `expert_ids`: each row names 8 different experts; in the 128 rows of one device no expert is named by more than 72 rows. `prefix_lengths`: some request has exactly 1024 cached tokens.
All inputs are finite; a program needn't handle non-finite values. No bound on the sum of `mask_positions` on one device may be relied on, other than what follows from the above.
Results may differ from a plain program's by a relative error of at most 0.017.
Values may be sent and summed in bfloat16 or wider, within the bound.
No kernel may reach another device: no remote copies, remote signals or barrier semaphores. Data moves between devices by JAX's collectives and lax.ppermute only.
A program may use at most 128 MiB of HBM per device.

v0:
```python
import functools
import math

import jax
import jax.numpy as jnp
from jax import lax
from jax.experimental import pallas as pl
from jax.experimental.pallas import tpu as pltpu
from jax.sharding import PartitionSpec as P

HD = 128
QB = 128
BF16 = jnp.bfloat16
F32 = jnp.float32
ROUTE = 128
MIB = 1024 * 1024
LIGHT = pl.CostEstimate(flops=1, bytes_accessed=1, transcendentals=0)


def params(mib):
    return pltpu.CompilerParams(vmem_limit_bytes=mib * MIB)


def attend_body(
    first,
    lens_ref,
    tok_ref,
    mask_ref,
    embed_ref,
    query_ref,
    new_key_ref,
    new_value_ref,
    key_ref,
    value_ref,
    gain_ref,
    ids_ref,
    probs_ref,
    resid_ref,
    normed_ref,
):
    block_len, width = tok_ref.shape
    prefix, kv_width = key_ref.shape[1:]
    kv_heads = kv_width // HD
    group = width // HD // kv_heads
    request = first + pl.program_id(0)
    length = lens_ref[request]
    scale = math.log2(math.e) / math.sqrt(HD)
    contract_last = (((1,), (1,)), ((), ()))
    queries = [
        jnp.concatenate(
            [query_ref[:, at * HD : (at + 1) * HD] for at in range(head * group, (head + 1) * group)],
            axis=0,
        )
        for head in range(kv_heads)
    ]

    def over(live):
        position = lax.broadcasted_iota(jnp.int32, (1, live), 1)
        closed = jnp.where(position < length, 0.0, -1e30)
        for head in range(kv_heads):
            lanes = slice(head * HD, (head + 1) * HD)
            query = queries[head]
            far = lax.dot_general(
                query, key_ref[0, :live, lanes], contract_last, preferred_element_type=F32
            )
            near = lax.dot_general(
                query, new_key_ref[:, lanes], contract_last, preferred_element_type=F32
            )
            far = far + closed
            top = jnp.maximum(
                jnp.max(far, axis=1, keepdims=True), jnp.max(near, axis=1, keepdims=True)
            )
            far = jnp.exp2((far - top) * scale)
            near = jnp.exp2((near - top) * scale)
            total = jnp.sum(far, axis=1, keepdims=True) + jnp.sum(near, axis=1, keepdims=True)
            out = jnp.dot(
                far.astype(BF16), value_ref[0, :live, lanes], preferred_element_type=F32
            )
            out = out + jnp.dot(
                near.astype(BF16), new_value_ref[:, lanes], preferred_element_type=F32
            )
            out = (out / total).astype(BF16).astype(F32)
            for g in range(group):
                at = (head * group + g) * HD
                resid_ref[:, at : at + HD] = out[g * block_len : (g + 1) * block_len]

    chunk = min(256, prefix)
    chunks = prefix // chunk
    needed = lax.div(length + (chunk - 1), chunk)
    for number in range(1, chunks + 1):
        low = needed <= number if number == 1 else needed == number

        @pl.when(low)
        def _():
            over(number * chunk)

    tok_rows = mask_ref.shape[0]
    row_at = lax.broadcasted_iota(jnp.int32, (block_len, tok_rows), 0) + request * block_len
    on_row = row_at == lax.broadcasted_iota(jnp.int32, (block_len, tok_rows), 1)
    probs = probs_ref[...]
    high = probs.astype(BF16).astype(F32)
    top_k = ids_ref.shape[0]
    table = jnp.concatenate(
        [
            ids_ref[...].astype(F32),
            high,
            probs - high,
            jnp.broadcast_to(mask_ref[...].reshape(1, tok_rows).astype(F32), (8, tok_rows)),
        ],
        axis=0,
    ).astype(BF16)
    table = lax.dot_general(
        on_row.astype(BF16), table, contract_last, preferred_element_type=F32
    )
    mask = table[:, 3 * top_k : 3 * top_k + 1]
    embed = embed_ref[...].reshape(1, width).astype(F32)
    gain = gain_ref[...].reshape(1, width).astype(F32)
    resid = jnp.where(mask > 0.5, embed, tok_ref[...].astype(F32)) + resid_ref[...]
    mean_square = jnp.mean(resid * resid, axis=1, keepdims=True)
    resid_ref[...] = resid
    normed_ref[:, :width] = (resid * lax.rsqrt(mean_square + 1e-06) * gain).astype(BF16)
    lane = lax.broadcasted_iota(jnp.int32, (block_len, ROUTE), 1)
    lane_id = (lane % (ROUTE // 2)).astype(F32)
    share = jnp.zeros((block_len, ROUTE), F32)
    for k in range(top_k):
        high, low = (table[:, at + k : at + k + 1] for at in (top_k, 2 * top_k))
        share = share + jnp.where(
            lane_id == table[:, k : k + 1], jnp.where(lane < ROUTE // 2, high, low), 0.0
        )
    normed_ref[:, width:] = share.astype(BF16)


def attend(first, count, lens, tokens, mask, embed, queries, new_keys, new_values, keys, values, gain, ids, probs):
    tok_rows, width = tokens.shape
    requests, prefix, kv_width = keys.shape
    block_len = tok_rows // requests

    def rows(cols):
        return pl.BlockSpec((block_len, cols), lambda i, lens: (first + i, 0))

    def cache():
        return pl.BlockSpec((1, prefix, kv_width), lambda i, lens: (first + i, 0, 0))

    def whole(size):
        return pl.BlockSpec((size,), lambda i, lens: (0,))

    def out(cols):
        return pl.BlockSpec((block_len, cols), lambda i, lens: (i, 0))

    scored = count * block_len * width * (prefix + block_len)
    return pl.pallas_call(
        functools.partial(attend_body, first),
        grid_spec=pltpu.PrefetchScalarGridSpec(
            num_scalar_prefetch=1,
            grid=(count,),
            in_specs=[
                rows(width),
                whole(tok_rows),
                whole(width),
                rows(width),
                rows(kv_width),
                rows(kv_width),
                cache(),
                cache(),
                whole(width),
                pl.BlockSpec(ids.shape, lambda i, lens: (0, 0)),
                pl.BlockSpec(ids.shape, lambda i, lens: (0, 0)),
            ],
            out_specs=[out(width), out(width + ROUTE)],
        ),
        out_shape=[
            jax.ShapeDtypeStruct((count * block_len, width), F32),
            jax.ShapeDtypeStruct((count * block_len, width + ROUTE), BF16),
        ],
        compiler_params=params(60 if first == 0 else 24),
        cost_estimate=LIGHT,
        name="attend",
    )(lens, tokens, mask, embed, queries, new_keys, new_values, keys, values, gain, ids, probs)


def scale_blocks(factor_of, quant_ref, out_ref, lead):
    row_count, col_count = quant_ref.shape[1:]
    start = pl.program_id(0) * row_count
    for i in range(row_count // QB):
        rows = pl.ds(pl.multiple_of(start + i * QB, QB), QB)
        for j in range(col_count // QB):
            cols = slice(j * QB, (j + 1) * QB)
            factor = factor_of(pl.program_id(0) * (row_count // QB) + i, j)
            block = quant_ref[0, i * QB : (i + 1) * QB, cols].astype(F32) * factor
            out_ref[(*lead, rows, cols)] = block.astype(BF16)


def dequant_body(gate_s, up_s, down_s, gate_ref, up_ref, down_ref, gate_up_ref, out_down_ref):
    scale_blocks(lambda i, j: gate_s[0, j, i], gate_ref, gate_up_ref, (0,))
    scale_blocks(lambda i, j: up_s[0, j, i], up_ref, gate_up_ref, (1,))
    scale_blocks(lambda i, j: down_s[0, i, j], down_ref, out_down_ref, ())


def dequant(gate, gate_scale, up, up_scale, down, down_scale):
    _, width, hidden = gate.shape
    steps = hidden // QB
    part, down_part = width // steps, hidden // steps
    smem = pl.BlockSpec(memory_space=pltpu.SMEM)
    vmem = pl.BlockSpec(memory_space=pltpu.VMEM)
    tall = pl.BlockSpec((1, part, hidden), lambda i: (0, i, 0))
    return pl.pallas_call(
        dequant_body,
        grid=(steps,),
        in_specs=[
            smem,
            smem,
            smem,
            tall,
            tall,
            pl.BlockSpec((1, down_part, width), lambda i: (0, i, 0)),
        ],
        out_specs=[vmem, vmem],
        out_shape=[
            jax.ShapeDtypeStruct((2, width, hidden), BF16),
            jax.ShapeDtypeStruct((hidden, width), BF16),
        ],
        compiler_params=params(8),
        cost_estimate=LIGHT,
        name="dequant",
    )(gate_scale, up_scale, down_scale, gate, up, down)


def experts_body(blocks, chip_ref, *refs):
    x_refs, refs = refs[:blocks], refs[blocks:]
    weight_refs, refs = refs[:4], refs[4:]
    out_refs, (x_all, total) = refs[:blocks], refs[blocks:]
    rows = x_refs[0].shape[0]
    width = x_all.shape[1]
    lane = lax.broadcasted_iota(jnp.int32, (rows, ROUTE), 1) % (ROUTE // 2)
    for at, ref in enumerate(x_refs):
        x_all[at * rows : (at + 1) * rows] = ref[:, :width]
    for number in range(2):
        gate_up, down = weight_refs[2 * number : 2 * number + 2]
        named = lane == chip_ref[number]
        shares = [jnp.where(named, ref[:, width:].astype(F32), 0.0) for ref in x_refs]
        share = jnp.sum(jnp.concatenate(shares, axis=0), axis=1, keepdims=True)
        hidden_width = down.shape[0]
        tile = min(256, hidden_width)
        for at in range(0, hidden_width, tile):
            cols = slice(at, at + tile)
            x = x_all[...]
            gate = jnp.dot(x, gate_up[0, :, cols], preferred_element_type=F32)
            up = jnp.dot(x, gate_up[1, :, cols], preferred_element_type=F32)
            hidden = (gate * jax.nn.sigmoid(gate) * up * share).astype(BF16)
            part = jnp.dot(hidden, down[cols, :], preferred_element_type=F32)
            if number == 0 and at == 0:
                total[...] = part
            else:
                total[...] += part
    for at, ref in enumerate(out_refs):
        ref[...] = total[at * rows : (at + 1) * rows].astype(BF16)


def experts(xs, chip, own, other):
    rows = xs[0].shape[0]
    width = own[1].shape[1]
    hidden = own[1].shape[0]
    blocks = len(xs)
    all_rows = rows * blocks
    vmem = pl.BlockSpec(memory_space=pltpu.VMEM)
    return pl.pallas_call(
        functools.partial(experts_body, blocks),
        in_specs=[pl.BlockSpec(memory_space=pltpu.SMEM)] + [vmem] * (blocks + 4),
        out_specs=[vmem] * blocks,
        out_shape=[jax.ShapeDtypeStruct((rows, width), BF16)] * blocks,
        scratch_shapes=[pltpu.VMEM((all_rows, width), BF16), pltpu.VMEM((all_rows, width), F32)],
        compiler_params=params(16),
        cost_estimate=LIGHT,
        name="experts",
    )(chip, *xs, *own, *other)


def add(*terms):
    total = terms[0].astype(F32)
    for term in terms[1:]:
        total = total + term.astype(F32)
    return total.astype(BF16)


def shards(
    sizes,
    tokens,
    mask_positions,
    mask_embed,
    queries,
    new_keys,
    new_values,
    cache_keys,
    cache_values,
    prefix_lengths,
    expert_ids,
    gate_probs,
    norm_gain,
    gate_quant,
    gate_scale,
    up_quant,
    up_scale,
    down_quant,
    down_scale,
):
    depth, side = sizes
    devices = depth * side * 2
    tok_rows, width = tokens.shape
    requests = cache_keys.shape[0]
    me = lax.axis_index("dp")

    def place(z, y, core):
        return (z * side + y) * 2 + core

    everyone = [(a, b, c) for a in range(depth) for b in range(side) for c in range(2)]
    next_chip = [(place(a, b, c), place((a + 1) % depth, b, c)) for a, b, c in everyone]
    other_side = [(place(a, b, c), place(a, side - 1 - b, c)) for a, b, c in everyone]
    other_core = [(place(a, b, c), place(a, b, 1 - c)) for a, b, c in everyone]

    def up(value):
        return lax.ppermute(value, "dp", next_chip)

    def across(value):
        return lax.ppermute(value, "dp", other_side)

    gate_scale, up_scale = jnp.swapaxes(gate_scale, 1, 2), jnp.swapaxes(up_scale, 1, 2)
    quantized = (gate_quant, gate_scale, up_quant, up_scale, down_quant, down_scale)
    from_core = [lax.ppermute(value, "dp", other_core) for value in quantized]
    chip = jnp.stack([me, me + 1 - 2 * (me % 2)])

    fixed = (
        prefix_lengths,
        tokens,
        mask_positions,
        mask_embed,
        queries,
        new_keys,
        new_values,
        cache_keys,
        cache_values,
        norm_gain,
        expert_ids.T,
        gate_probs.T,
    )
    if side == 1:
        resid, normed = attend(0, requests, *fixed)
        own, other = dequant(*quantized), dequant(*from_core)
        (near,) = experts([normed], chip, own, other)

        def turn(_, carry):
            block, sums = carry
            block = up(block)
            (part,) = experts([block], chip, own, other)
            return block, add(up(sums), part)

        _, sums = lax.fori_loop(1, depth, turn, (normed, jnp.zeros_like(near)))
        return (resid + near.astype(F32) + up(sums).astype(F32)).astype(BF16)

    halves = 2
    count = requests // halves
    last = halves - 1
    latest = []

    def after(values):
        return lax.optimization_barrier((values, latest[-1]))[0] if latest else values

    def then(function, *values):
        out = function(*after(values))
        latest.append(jax.tree.leaves(out)[0])
        return out

    resids, rows_of, sides_of, parts, sums = {}, {}, {}, {}, {}

    def run_attend(half):
        lens = fixed[0]
        resids[half], normed = then(
            lambda lens: attend(half * count, count, lens, *fixed[1:]), lens
        )
        rows_of[0, half] = normed

    def send(back, half):
        rows = after(rows_of[back, half])
        rows_of[back, half] = rows
        if back < depth - 1:
            rows_of[back + 1, half] = up(rows)
        if (back, half) != (depth - 1, last):
            sides_of[back, half] = across(rows)
        if (back, half) == (depth - 2, last):
            sides_of[back, half] = after(sides_of[back, half])
            sides_of[back + 1, half] = up(sides_of[back, half])

    def run_dequant(values):
        return then(lambda scale: dequant(*values[:5], scale), values[5])

    def run_experts(back, half):
        here, there = then(
            lambda x: experts([x, sides_of[back, half]], chip, own, other), rows_of[back, half]
        )
        if (back, half) == (1, last):
            parts[back, half] = [here]
            sums["held"] = up(there)
        else:
            if (back, half) == (2, last):
                there = then(add, there, sums["held"])
            parts[back, half] = [here, across(there)]

    def run_add(back, half):
        terms = parts[back, half]
        if back != 1:
            terms = terms + [sums[half]]
        if back == 0:
            terms = [resids[half]] + terms
        sums[half] = then(add, *terms)
        if back != 0:
            sums[half] = up(sums[half])

    run_attend(0)
    send(0, 0)
    run_attend(1)
    send(0, 1)
    own = run_dequant(quantized)
    send(1, 0)
    other = run_dequant(from_core)
    send(1, 1)
    send(2, 0)
    run_experts(1, 0)
    send(2, 1)
    run_experts(1, 1)
    send(3, 0)
    run_experts(2, 0)
    run_add(1, 0)
    run_experts(2, 1)
    run_add(1, 1)
    run_experts(3, 0)
    run_add(2, 0)
    run_experts(3, 1)
    run_add(2, 1)
    run_experts(0, 0)
    run_add(3, 0)
    run_experts(0, 1)
    run_add(3, 1)
    run_add(0, 0)
    run_add(0, 1)
    return jnp.concatenate([sums[half] for half in range(halves)], 0)


def solution(mesh):
    in_specs = (
        P(("groups", "dp"), None),
        P(("groups", "dp")),
        P(),
        P(("groups", "dp"), None),
        P(("groups", "dp"), None),
        P(("groups", "dp"), None),
        P(("groups", "dp"), None, None),
        P(("groups", "dp"), None, None),
        P(("groups", "dp")),
        P(("groups", "dp"), None),
        P(("groups", "dp"), None),
        P(),
        P("dp", None, None),
        P("dp", None, None),
        P("dp", None, None),
        P("dp", None, None),
        P("dp", None, None),
        P("dp", None, None),
    )
    out_specs = P(("groups", "dp"), None)
    chips = mesh.shape["dp"] // 2
    sizes = (chips // 2, 2) if chips == 8 else (chips, 1)
    return jax.shard_map(
        functools.partial(shards, sizes),
        mesh=mesh,
        in_specs=in_specs,
        out_specs=out_specs,
        check_vma=False,
    )
```

profile of v0, /device:TPU:0, one launch (start us, length us, event | category | flops | bytes accessed | tf_op | source)
XLA Modules:
  0.0 115.8 jit_solution(15841523674879174053)
XLA Ops:
  1.1 5.2 %attend.2 = (f32[64,2048]{1,0:T(8,128)}, bf16[64,2176]{1,0:T(8,128)(2,1)}) custom-call(s32[4]{0:T(128)} %lens_ref.2, bf16[128,2048]{1,0:T(8,128)(2,1)} %tok_ref.3, s32[128]{0:T(128)} %mask_ref.3, bf16[2048]{0:T(1024)(128)(2,1)} %embed_ref.3, bf16[128,2048]{1,0:T(8,128)(2,1)} %query_ref.3, bf16[128,256]{1,0:T(8,128)(2,1)} %new_key_ref.3, ...), custom_call_target="tpu_custom_call" | custom-call | flops 1 | bytes 1 | tf_op jit(solution)/shard_map/attend/pallas_call | solution.py:151
  6.2 2.6 %collective-permute-start.8 = (bf16[64,2176]{1,0:T(8,128)(2,1)}, bf16[64,2176]{1,0:T(8,128)(2,1)}, u32[]{:S(2)}, u32[]{:S(2)}) collective-permute-start(bf16[64,2176]{1,0:T(8,128)(2,1)} %get-tuple-element.119.refs_0_), channel_id=1, source_target_pairs={{0,4},{1,5},{2,6},{3,7},{4,8},{5,9},{6,10},{7,11},{8,12},{9,13},{1... | collective-permute-start | bytes 835592 | tf_op jit(solution)/shard_map/ppermute | solution.py:321
  10.8 2.7 %attend.3 = (f32[64,2048]{1,0:T(8,128)S(1)}, bf16[64,2176]{1,0:T(8,128)(2,1)S(1)}) custom-call(s32[4]{0:T(128)S(1)} %copy-done.19, bf16[128,2048]{1,0:T(8,128)(2,1)S(1)} %copy-done.7, s32[128]{0:T(128)S(1)} %copy-done.20, bf16[2048]{0:T(1024)(128)(2,1)S(1)} %copy-done.12, bf16[128,2048]{1,0:T(8,128)(2,1)S(1)} %copy-done.8, bf16[128,256]{1,0:T(8,128)(2,1)S(1)} %copy-done.10, ...), custom_call_target="tpu_custom_call" | custom-call | flops 1 | bytes 1 | tf_op jit(solution)/shard_map/attend/pallas_call | solution.py:151
  15.7 3.1 %collective-permute-done.8.refs_0_ = bf16[64,2176]{1,0:T(8,128)(2,1)} collective-permute-done((bf16[64,2176]{1,0:T(8,128)(2,1)}, bf16[64,2176]{1,0:T(8,128)(2,1)}, u32[]{:S(2)}, u32[]{:S(2)}) %collective-permute-start.8) | collective-permute-done | bytes 278560 | tf_op jit(solution)/shard_map/ppermute | solution.py:321
  20.3 2.4 %dequant.2 = (bf16[2,2048,512]{2,1,0:T(8,128)(2,1)S(1)}, bf16[512,2048]{1,0:T(8,128)(2,1)S(1)}) custom-call(f32[1,4,16]{2,1,0:T(4,128)S(1)} %bitcast.11, f32[1,4,16]{2,1,0:T(4,128)S(1)} %bitcast.13, f32[1,4,16]{2,1,0:T(4,128)S(1)} %copy-done.17, bf16[1,2048,512]{2,1,0:T(8,128)(2,1)S(1)} %copy-done.4, bf16[1,2048,512]{2,1,0:T(8,128)(2,1)S(1)} %copy-done.5, ...), custom_call_target="tpu_custom_call" | custom-call | flops 1 | bytes 1 | tf_op jit(solution)/shard_map/dequant/pallas_call | solution.py:206
  27.6 4.5 %dequant.3 = (bf16[2,2048,512]{2,1,0:T(8,128)(2,1)S(1)}, bf16[512,2048]{1,0:T(8,128)(2,1)S(1)}) custom-call(f32[1,4,16]{2,1,0:T(4,128)S(1)} %collective-permute-done.1.gate_s, f32[1,4,16]{2,1,0:T(4,128)S(1)} %collective-permute-done.2.up_s, f32[1,4,16]{2,1,0:T(4,128)S(1)} %collective-permute-done.3.down_s, ...), custom_call_target="tpu_custom_call" | custom-call | flops 1 | bytes 1 | tf_op jit(solution)/shard_map/dequant/pallas_call | solution.py:206
  37.3 3.4 %experts.8 = (bf16[64,2048]{1,0:T(8,128)(2,1)S(1)}, bf16[64,2048]{1,0:T(8,128)(2,1)S(1)}) custom-call(s32[2]{0:T(128)S(1)} %pad_add_fusion.chip_ref, bf16[64,2176]{1,0:T(8,128)(2,1)} %collective-permute-done.8.refs_0_, bf16[64,2176]{1,0:T(8,128)(2,1)S(1)} %collective-permute-done.9.refs_1_, bf16[2,2048,512]{2,1,0:T(8,128)(2,1)S(1)} %copy-done.1, ...), custom_call_target="tpu_custom_call" | custom-call | flops 1 | bytes 1 | tf_op jit(solution)/shard_map/experts/pallas_call | solution.py:266
  44.4 3.4 %experts.9 = (bf16[64,2048]{1,0:T(8,128)(2,1)S(1)}, bf16[64,2048]{1,0:T(8,128)(2,1)S(1)}) custom-call(s32[2]{0:T(128)S(1)} %pad_add_fusion.chip_ref, bf16[64,2176]{1,0:T(8,128)(2,1)} %collective-permute-done.refs_0_, bf16[64,2176]{1,0:T(8,128)(2,1)S(1)} %collective-permute-done.12.refs_1_, bf16[2,2048,512]{2,1,0:T(8,128)(2,1)S(1)} %copy-done.1, ...), custom_call_target="tpu_custom_call" | custom-call | flops 1 | bytes 1 | tf_op jit(solution)/shard_map/experts/pallas_call | solution.py:266
  49.8 3.4 %experts.10 = (bf16[64,2048]{1,0:T(8,128)(2,1)S(1)}, bf16[64,2048]{1,0:T(8,128)(2,1)S(1)}) custom-call(s32[2]{0:T(128)S(1)} %pad_add_fusion.chip_ref, bf16[64,2176]{1,0:T(8,128)(2,1)} %collective-permute-done.11.refs_0_, bf16[64,2176]{1,0:T(8,128)(2,1)S(1)} %collective-permute-done.13.refs_1_, bf16[2,2048,512]{2,1,0:T(8,128)(2,1)S(1)} %copy-done.1, ...), custom_call_target="tpu_custom_call" | custom-call | flops 1 | bytes 1 | tf_op jit(solution)/shard_map/experts/pallas_call | solution.py:266
  53.1 2.2 %collective-permute-done.10 = bf16[64,2048]{1,0:T(8,128)(2,1)S(1)} collective-permute-done((bf16[64,2048]{1,0:T(8,128)(2,1)S(1)}, bf16[64,2048]{1,0:T(8,128)(2,1)S(1)}, u32[]{:S(2)}, u32[]{:S(2)}) %collective-permute-start.10) | collective-permute-done | bytes 262176 | tf_op jit(solution)/shard_map/ppermute | solution.py:324
  55.4 2.1 %collective-permute-start.15 = (bf16[64,2048]{1,0:T(8,128)(2,1)S(1)}, bf16[64,2048]{1,0:T(8,128)(2,1)S(1)}, u32[]{:S(2)}, u32[]{:S(2)}) collective-permute-start(bf16[64,2048]{1,0:T(8,128)(2,1)S(1)} %get-tuple-element.103), channel_id=1, source_target_pairs={{0,4},{1,5},{2,6},{3,7},{4,8},{5,9},{6,10},{7,11},{8,12},{9,13},{1... | collective-permute-start | bytes 786440 | tf_op jit(solution)/shard_map/ppermute | solution.py:321
  58.6 5.7 %collective-permute-done.14.refs_1_ = bf16[64,2176]{1,0:T(8,128)(2,1)S(1)} collective-permute-done((bf16[64,2176]{1,0:T(8,128)(2,1)S(1)}, bf16[64,2176]{1,0:T(8,128)(2,1)S(1)}, u32[]{:S(2)}, u32[]{:S(2)}) %collective-permute-start.14) | collective-permute-done | bytes 278560 | tf_op jit(solution)/shard_map/ppermute | solution.py:324
  65.8 2.9 %experts.11 = (bf16[64,2048]{1,0:T(8,128)(2,1)S(1)}, bf16[64,2048]{1,0:T(8,128)(2,1)S(1)}) custom-call(s32[2]{0:T(128)S(1)} %pad_add_fusion.chip_ref, bf16[64,2176]{1,0:T(8,128)(2,1)S(1)} %collective-permute-done.7.refs_0_, bf16[64,2176]{1,0:T(8,128)(2,1)S(1)} %collective-permute-done.14.refs_1_, bf16[2,2048,512]{2,1,0:T(8,128)(2,1)S(1)} %copy-done.1, ...), custom_call_target="tpu_custom_call" | custom-call | flops 1 | bytes 1 | tf_op jit(solution)/shard_map/experts/pallas_call | solution.py:266
  69.4 3.3 %collective-permute-done.22.refs_1_ = bf16[64,2176]{1,0:T(8,128)(2,1)S(1)} collective-permute-done((bf16[64,2176]{1,0:T(8,128)(2,1)S(1)}, bf16[64,2176]{1,0:T(8,128)(2,1)S(1)}, u32[]{:S(2)}, u32[]{:S(2)}) %collective-permute-start.22) | collective-permute-done | bytes 278560 | tf_op jit(solution)/shard_map/ppermute | solution.py:324
  72.7 2.8 %collective-permute-start.23 = (bf16[64,2176]{1,0:T(8,128)(2,1)S(1)}, bf16[64,2176]{1,0:T(8,128)(2,1)S(1)}, u32[]{:S(2)}, u32[]{:S(2)}) collective-permute-start(bf16[64,2176]{1,0:T(8,128)(2,1)S(1)} %collective-permute-done.14.refs_1_), channel_id=1, source_target_pairs={{0,4},{1,5},{2,6},{3,7},{4,8},{5,9},{6,10},{7,11},{8,12},{9,13},{1... | collective-permute-start | bytes 835592 | tf_op jit(solution)/shard_map/ppermute | solution.py:321
  75.5 2.9 %experts.12 = (bf16[64,2048]{1,0:T(8,128)(2,1)S(1)}, bf16[64,2048]{1,0:T(8,128)(2,1)S(1)}) custom-call(s32[2]{0:T(128)S(1)} %pad_add_fusion.chip_ref, bf16[64,2176]{1,0:T(8,128)(2,1)S(1)} %collective-permute-done.21.refs_0_, bf16[64,2176]{1,0:T(8,128)(2,1)S(1)} %collective-permute-done.22.refs_1_, bf16[2,2048,512]{2,1,0:T(8,128)(2,1)S(1)} %copy-done.1, ...), custom_call_target="tpu_custom_call" | custom-call | flops 1 | bytes 1 | tf_op jit(solution)/shard_map/experts/pallas_call | solution.py:266
  78.9 2.3 %collective-permute-start.16 = (bf16[64,2048]{1,0:T(8,128)(2,1)S(1)}, bf16[64,2048]{1,0:T(8,128)(2,1)S(1)}, u32[]{:S(2)}, u32[]{:S(2)}) collective-permute-start(bf16[64,2048]{1,0:T(8,128)(2,1)S(1)} %add_convert_fusion.6), channel_id=1, source_target_pairs={{0,2},{1,3},{2,0},{3,1},{4,6},{5,7},{6,4},{7,5},{8,10},{9,11},{10,... | collective-permute-start | bytes 786440 | tf_op jit(solution)/shard_map/ppermute | solution.py:324
  81.4 2.6 %collective-permute-done.23.refs_1_ = bf16[64,2176]{1,0:T(8,128)(2,1)S(1)} collective-permute-done((bf16[64,2176]{1,0:T(8,128)(2,1)S(1)}, bf16[64,2176]{1,0:T(8,128)(2,1)S(1)}, u32[]{:S(2)}, u32[]{:S(2)}) %collective-permute-start.23) | collective-permute-done | bytes 278560 | tf_op jit(solution)/shard_map/ppermute | solution.py:321
  85.1 2.9 %experts.13 = (bf16[64,2048]{1,0:T(8,128)(2,1)S(1)}, bf16[64,2048]{1,0:T(8,128)(2,1)S(1)}) custom-call(s32[2]{0:T(128)S(1)} %pad_add_fusion.chip_ref, bf16[64,2176]{1,0:T(8,128)(2,1)S(1)} %collective-permute-done.18.refs_0_, bf16[64,2176]{1,0:T(8,128)(2,1)S(1)} %collective-permute-done.23.refs_1_, bf16[2,2048,512]{2,1,0:T(8,128)(2,1)S(1)} %copy-done.1, ...), custom_call_target="tpu_custom_call" | custom-call | flops 1 | bytes 1 | tf_op jit(solution)/shard_map/experts/pallas_call | solution.py:266
  92.5 2.9 %experts.14 = (bf16[64,2048]{1,0:T(8,128)(2,1)S(1)}, bf16[64,2048]{1,0:T(8,128)(2,1)S(1)}) custom-call(s32[2]{0:T(128)S(1)} %pad_add_fusion.chip_ref, bf16[64,2176]{1,0:T(8,128)(2,1)S(1)} %copy-done.9, bf16[64,2176]{1,0:T(8,128)(2,1)S(1)} %collective-permute-done.24.refs_1_, bf16[2,2048,512]{2,1,0:T(8,128)(2,1)S(1)} %copy-done.1, ...), custom_call_target="tpu_custom_call" | custom-call | flops 1 | bytes 1 | tf_op jit(solution)/shard_map/experts/pallas_call | solution.py:266
  95.5 3.4 %collective-permute-done.26 = bf16[64,2048]{1,0:T(8,128)(2,1)S(1)} collective-permute-done((bf16[64,2048]{1,0:T(8,128)(2,1)S(1)}, bf16[64,2048]{1,0:T(8,128)(2,1)S(1)}, u32[]{:S(2)}, u32[]{:S(2)}) %collective-permute-start.26) | collective-permute-done | bytes 262176 | tf_op jit(solution)/shard_map/ppermute | solution.py:324
  101.5 2.9 %experts.15 = (bf16[64,2048]{1,0:T(8,128)(2,1)S(1)}, bf16[64,2048]{1,0:T(8,128)(2,1)S(1)}) custom-call(s32[2]{0:T(128)S(1)} %pad_add_fusion.chip_ref, bf16[64,2176]{1,0:T(8,128)(2,1)S(1)} %get-tuple-element.127.refs_0_, bf16[64,2176]{1,0:T(8,128)(2,1)S(1)} %collective-permute-done.31.refs_1_, bf16[2,2048,512]{2,1,0:T(8,128)(2,1)S(1)} %copy-done.1, ...), custom_call_target="tpu_custom_call" | custom-call | flops 1 | bytes 1 | tf_op jit(solution)/shard_map/experts/pallas_call | solution.py:266
  109.4 2.7 %collective-permute-done.32 = bf16[64,2048]{1,0:T(8,128)(2,1)S(1)} collective-permute-done((bf16[64,2048]{1,0:T(8,128)(2,1)S(1)}, bf16[64,2048]{1,0:T(8,128)(2,1)S(1)}, u32[]{:S(2)}, u32[]{:S(2)}) %collective-permute-start.32) | collective-permute-done | bytes 262176 | tf_op jit(solution)/shard_map/ppermute | solution.py:324
  112.1 2.7 %collective-permute-done.33 = bf16[64,2048]{1,0:T(8,128)(2,1)S(1)} collective-permute-done((bf16[64,2048]{1,0:T(8,128)(2,1)S(1)}, bf16[64,2048]{1,0:T(8,128)(2,1)S(1)}, u32[]{:S(2)}, u32[]{:S(2)}) %collective-permute-start.33) | collective-permute-done | bytes 262176 | tf_op jit(solution)/shard_map/ppermute | solution.py:321
  (110 shorter events, 40.3 us)
Async XLA Ops:
  0.0 25.8 %collective-permute-start.4 = (bf16[1,2048,512]{2,1,0:T(8,128)(2,1)}, bf16[1,2048,512]{2,1,0:T(8,128)(2,1)}, u32[]{:S(2)}, u32[]{:S(2)}) collective-permute-start(bf16[1,2048,512]{2,1,0:T(8,128)(2,1)} %gate_ref.1), channel_id=1, source_target_pairs={{0,1},{1,0},{2,3},{3,2},{4,5},{5,4},{6,7},{7,6},{8,9},{9,8},{10,11... | collective-permute-start | bytes 6291464 | tf_op jit(solution)/shard_map/ppermute | solution.py:328
  0.5 27.1 %collective-permute-start.5 = (bf16[1,2048,512]{2,1,0:T(8,128)(2,1)}, bf16[1,2048,512]{2,1,0:T(8,128)(2,1)}, u32[]{:S(2)}, u32[]{:S(2)}) collective-permute-start(bf16[1,2048,512]{2,1,0:T(8,128)(2,1)} %up_ref.1), channel_id=1, source_target_pairs={{0,1},{1,0},{2,3},{3,2},{4,5},{5,4},{6,7},{7,6},{8,9},{9,8},{10,11... | collective-permute-start | bytes 6291464 | tf_op jit(solution)/shard_map/ppermute | solution.py:328
  0.5 27.0 %collective-permute-start.6 = (bf16[1,512,2048]{2,1,0:T(8,128)(2,1)}, bf16[1,512,2048]{2,1,0:T(8,128)(2,1)}, u32[]{:S(2)}, u32[]{:S(2)}) collective-permute-start(bf16[1,512,2048]{2,1,0:T(8,128)(2,1)} %down_ref.1), channel_id=1, source_target_pairs={{0,1},{1,0},{2,3},{3,2},{4,5},{5,4},{6,7},{7,6},{8,9},{9,8},{10,11... | collective-permute-start | bytes 6291464 | tf_op jit(solution)/shard_map/ppermute | solution.py:328
  6.2 12.5 %collective-permute-start.8 = (bf16[64,2176]{1,0:T(8,128)(2,1)}, bf16[64,2176]{1,0:T(8,128)(2,1)}, u32[]{:S(2)}, u32[]{:S(2)}) collective-permute-start(bf16[64,2176]{1,0:T(8,128)(2,1)} %get-tuple-element.119.refs_0_), channel_id=1, source_target_pairs={{0,4},{1,5},{2,6},{3,7},{4,8},{5,9},{6,10},{7,11},{8,12},{9,13},{1... | collective-permute-start | bytes 835592 | tf_op jit(solution)/shard_map/ppermute | solution.py:321
  18.7 13.3 %collective-permute-start = (bf16[64,2176]{1,0:T(8,128)(2,1)S(1)}, bf16[64,2176]{1,0:T(8,128)(2,1)}, u32[]{:S(2)}, u32[]{:S(2)}) collective-permute-start(bf16[64,2176]{1,0:T(8,128)(2,1)S(1)} %get-tuple-element.127.refs_0_), channel_id=1, source_target_pairs={{0,4},{1,5},{2,6},{3,7},{4,8},{5,9},{6,10},{7,11},{8,12},{9,13},{1... | collective-permute-start | bytes 835592 | tf_op jit(solution)/shard_map/ppermute | solution.py:321
  24.7 10.8 %collective-permute-start.11 = (bf16[64,2176]{1,0:T(8,128)(2,1)}, bf16[64,2176]{1,0:T(8,128)(2,1)}, u32[]{:S(2)}, u32[]{:S(2)}) collective-permute-start(bf16[64,2176]{1,0:T(8,128)(2,1)} %collective-permute-done.8.refs_0_), channel_id=1, source_target_pairs={{0,4},{1,5},{2,6},{3,7},{4,8},{5,9},{6,10},{7,11},{8,12},{9,13},{1... | collective-permute-start | bytes 835592 | tf_op jit(solution)/shard_map/ppermute | solution.py:321
  25.8 11.5 %collective-permute-start.9 = (bf16[64,2176]{1,0:T(8,128)(2,1)}, bf16[64,2176]{1,0:T(8,128)(2,1)S(1)}, u32[]{:S(2)}, u32[]{:S(2)}) collective-permute-start(bf16[64,2176]{1,0:T(8,128)(2,1)} %collective-permute-done.8.refs_0_), channel_id=1, source_target_pairs={{0,2},{1,3},{2,0},{3,1},{4,6},{5,7},{6,4},{7,5},{8,10},{9,11},{10,... | collective-permute-start | bytes 835592 | tf_op jit(solution)/shard_map/ppermute | solution.py:324
  32.1 10.7 %collective-permute-start.7 = (bf16[64,2176]{1,0:T(8,128)(2,1)}, bf16[64,2176]{1,0:T(8,128)(2,1)S(1)}, u32[]{:S(2)}, u32[]{:S(2)}) collective-permute-start(bf16[64,2176]{1,0:T(8,128)(2,1)} %collective-permute-done.refs_0_), channel_id=1, source_target_pairs={{0,4},{1,5},{2,6},{3,7},{4,8},{5,9},{6,10},{7,11},{8,12},{9,13},{1... | collective-permute-start | bytes 835592 | tf_op jit(solution)/shard_map/ppermute | solution.py:321
  34.0 9.8 %collective-permute-start.12 = (bf16[64,2176]{1,0:T(8,128)(2,1)}, bf16[64,2176]{1,0:T(8,128)(2,1)S(1)}, u32[]{:S(2)}, u32[]{:S(2)}) collective-permute-start(bf16[64,2176]{1,0:T(8,128)(2,1)} %collective-permute-done.refs_0_), channel_id=1, source_target_pairs={{0,2},{1,3},{2,0},{3,1},{4,6},{5,7},{6,4},{7,5},{8,10},{9,11},{10,... | collective-permute-start | bytes 835592 | tf_op jit(solution)/shard_map/ppermute | solution.py:324
  35.5 14.2 %collective-permute-start.13 = (bf16[64,2176]{1,0:T(8,128)(2,1)}, bf16[64,2176]{1,0:T(8,128)(2,1)S(1)}, u32[]{:S(2)}, u32[]{:S(2)}) collective-permute-start(bf16[64,2176]{1,0:T(8,128)(2,1)} %collective-permute-done.11.refs_0_), channel_id=1, source_target_pairs={{0,2},{1,3},{2,0},{3,1},{4,6},{5,7},{6,4},{7,5},{8,10},{9,11},{10,... | collective-permute-start | bytes 835592 | tf_op jit(solution)/shard_map/ppermute | solution.py:324
  40.7 14.7 %collective-permute-start.10 = (bf16[64,2048]{1,0:T(8,128)(2,1)S(1)}, bf16[64,2048]{1,0:T(8,128)(2,1)S(1)}, u32[]{:S(2)}, u32[]{:S(2)}) collective-permute-start(bf16[64,2048]{1,0:T(8,128)(2,1)S(1)} %get-tuple-element.91), channel_id=1, source_target_pairs={{0,2},{1,3},{2,0},{3,1},{4,6},{5,7},{6,4},{7,5},{8,10},{9,11},{10,... | collective-permute-start | bytes 786440 | tf_op jit(solution)/shard_map/ppermute | solution.py:324
  41.1 51.4 %collective-permute-start.24 = (bf16[64,2176]{1,0:T(8,128)(2,1)S(1)}, bf16[64,2176]{1,0:T(8,128)(2,1)S(1)}, u32[]{:S(2)}, u32[]{:S(2)}) collective-permute-start(bf16[64,2176]{1,0:T(8,128)(2,1)S(1)} %copy-done.9), channel_id=1, source_target_pairs={{0,2},{1,3},{2,0},{3,1},{4,6},{5,7},{6,4},{7,5},{8,10},{9,11},{10,... | collective-permute-start | bytes 835592 | tf_op jit(solution)/shard_map/ppermute | solution.py:324
  42.8 14.9 %collective-permute-start.21 = (bf16[64,2176]{1,0:T(8,128)(2,1)}, bf16[64,2176]{1,0:T(8,128)(2,1)S(1)}, u32[]{:S(2)}, u32[]{:S(2)}) collective-permute-start(bf16[64,2176]{1,0:T(8,128)(2,1)} %collective-permute-done.11.refs_0_), channel_id=1, source_target_pairs={{0,4},{1,5},{2,6},{3,7},{4,8},{5,9},{6,10},{7,11},{8,12},{9,13},{1... | collective-permute-start | bytes 835592 | tf_op jit(solution)/shard_map/ppermute | solution.py:321
  43.8 20.5 %collective-permute-start.14 = (bf16[64,2176]{1,0:T(8,128)(2,1)S(1)}, bf16[64,2176]{1,0:T(8,128)(2,1)S(1)}, u32[]{:S(2)}, u32[]{:S(2)}) collective-permute-start(bf16[64,2176]{1,0:T(8,128)(2,1)S(1)} %collective-permute-done.7.refs_0_), channel_id=1, source_target_pairs={{0,2},{1,3},{2,0},{3,1},{4,6},{5,7},{6,4},{7,5},{8,10},{9,11},{10,... | collective-permute-start | bytes 835592 | tf_op jit(solution)/shard_map/ppermute | solution.py:324
  55.4 13.4 %collective-permute-start.15 = (bf16[64,2048]{1,0:T(8,128)(2,1)S(1)}, bf16[64,2048]{1,0:T(8,128)(2,1)S(1)}, u32[]{:S(2)}, u32[]{:S(2)}) collective-permute-start(bf16[64,2048]{1,0:T(8,128)(2,1)S(1)} %get-tuple-element.103), channel_id=1, source_target_pairs={{0,4},{1,5},{2,6},{3,7},{4,8},{5,9},{6,10},{7,11},{8,12},{9,13},{1... | collective-permute-start | bytes 786440 | tf_op jit(solution)/shard_map/ppermute | solution.py:321
  57.5 20.9 %collective-permute-start.20 = (bf16[64,2048]{1,0:T(8,128)(2,1)S(1)}, bf16[64,2048]{1,0:T(8,128)(2,1)S(1)}, u32[]{:S(2)}, u32[]{:S(2)}) collective-permute-start(bf16[64,2048]{1,0:T(8,128)(2,1)S(1)} %add_convert_fusion.7), channel_id=1, source_target_pairs={{0,4},{1,5},{2,6},{3,7},{4,8},{5,9},{6,10},{7,11},{8,12},{9,13},{1... | collective-permute-start | bytes 786440 | tf_op jit(solution)/shard_map/ppermute | solution.py:321
  57.7 23.7 %collective-permute-start.18 = (bf16[64,2176]{1,0:T(8,128)(2,1)S(1)}, bf16[64,2176]{1,0:T(8,128)(2,1)S(1)}, u32[]{:S(2)}, u32[]{:S(2)}) collective-permute-start(bf16[64,2176]{1,0:T(8,128)(2,1)S(1)} %collective-permute-done.7.refs_0_), channel_id=1, source_target_pairs={{0,4},{1,5},{2,6},{3,7},{4,8},{5,9},{6,10},{7,11},{8,12},{9,13},{1... | collective-permute-start | bytes 835592 | tf_op jit(solution)/shard_map/ppermute | solution.py:321
  68.8 10.1 %collective-permute-start.19 = (bf16[64,2048]{1,0:T(8,128)(2,1)S(1)}, bf16[64,2048]{1,0:T(8,128)(2,1)S(1)}, u32[]{:S(2)}, u32[]{:S(2)}) collective-permute-start(bf16[64,2048]{1,0:T(8,128)(2,1)S(1)} %get-tuple-element.107), channel_id=1, source_target_pairs={{0,2},{1,3},{2,0},{3,1},{4,6},{5,7},{6,4},{7,5},{8,10},{9,11},{10,... | collective-permute-start | bytes 786440 | tf_op jit(solution)/shard_map/ppermute | solution.py:324
  72.7 11.3 %collective-permute-start.23 = (bf16[64,2176]{1,0:T(8,128)(2,1)S(1)}, bf16[64,2176]{1,0:T(8,128)(2,1)S(1)}, u32[]{:S(2)}, u32[]{:S(2)}) collective-permute-start(bf16[64,2176]{1,0:T(8,128)(2,1)S(1)} %collective-permute-done.14.refs_1_), channel_id=1, source_target_pairs={{0,4},{1,5},{2,6},{3,7},{4,8},{5,9},{6,10},{7,11},{8,12},{9,13},{1... | collective-permute-start | bytes 835592 | tf_op jit(solution)/shard_map/ppermute | solution.py:321
  78.5 11.2 %collective-permute-start.17 = (bf16[64,2048]{1,0:T(8,128)(2,1)S(1)}, bf16[64,2048]{1,0:T(8,128)(2,1)S(1)}, u32[]{:S(2)}, u32[]{:S(2)}) collective-permute-start(bf16[64,2048]{1,0:T(8,128)(2,1)S(1)} %get-tuple-element.106), channel_id=1, source_target_pairs={{0,4},{1,5},{2,6},{3,7},{4,8},{5,9},{6,10},{7,11},{8,12},{9,13},{1... | collective-permute-start | bytes 786440 | tf_op jit(solution)/shard_map/ppermute | solution.py:321
  78.9 12.4 %collective-permute-start.16 = (bf16[64,2048]{1,0:T(8,128)(2,1)S(1)}, bf16[64,2048]{1,0:T(8,128)(2,1)S(1)}, u32[]{:S(2)}, u32[]{:S(2)}) collective-permute-start(bf16[64,2048]{1,0:T(8,128)(2,1)S(1)} %add_convert_fusion.6), channel_id=1, source_target_pairs={{0,2},{1,3},{2,0},{3,1},{4,6},{5,7},{6,4},{7,5},{8,10},{9,11},{10,... | collective-permute-start | bytes 786440 | tf_op jit(solution)/shard_map/ppermute | solution.py:324
  81.4 20.1 %collective-permute-start.31 = (bf16[64,2176]{1,0:T(8,128)(2,1)S(1)}, bf16[64,2176]{1,0:T(8,128)(2,1)S(1)}, u32[]{:S(2)}, u32[]{:S(2)}) collective-permute-start(bf16[64,2176]{1,0:T(8,128)(2,1)S(1)} %get-tuple-element.127.refs_0_), channel_id=1, source_target_pairs={{0,2},{1,3},{2,0},{3,1},{4,6},{5,7},{6,4},{7,5},{8,10},{9,11},{10,... | collective-permute-start | bytes 835592 | tf_op jit(solution)/shard_map/ppermute | solution.py:324
  84.1 11.4 %collective-permute-start.27 = (bf16[64,2048]{1,0:T(8,128)(2,1)S(1)}, bf16[64,2048]{1,0:T(8,128)(2,1)S(1)}, u32[]{:S(2)}, u32[]{:S(2)}) collective-permute-start(bf16[64,2048]{1,0:T(8,128)(2,1)S(1)} %add_convert_fusion.5), channel_id=1, source_target_pairs={{0,4},{1,5},{2,6},{3,7},{4,8},{5,9},{6,10},{7,11},{8,12},{9,13},{1... | collective-permute-start | bytes 786440 | tf_op jit(solution)/shard_map/ppermute | solution.py:321
  91.4 15.1 %collective-permute-start.30 = (bf16[64,2048]{1,0:T(8,128)(2,1)S(1)}, bf16[64,2048]{1,0:T(8,128)(2,1)S(1)}, u32[]{:S(2)}, u32[]{:S(2)}) collective-permute-start(bf16[64,2048]{1,0:T(8,128)(2,1)S(1)} %add_convert_fusion.4), channel_id=1, source_target_pairs={{0,4},{1,5},{2,6},{3,7},{4,8},{5,9},{6,10},{7,11},{8,12},{9,13},{1... | collective-permute-start | bytes 786440 | tf_op jit(solution)/shard_map/ppermute | solution.py:321
  (32 other events, 219.9 us)
where the time goes:
time: 117 us; the launch traced here: 116 us
  Pallas kernels  39.6 us (34%)
  starting transfers between devices  36.5 us (31%)
  waiting for transfers between devices  32.4 us (28%)
  local copies, waits for them, and re-layouts  5.22 us (4%)
  other arithmetic  1.69 us (1%)
    pallas_call x8, Pallas kernels, experts(): pl.pallas_call(functools.partial(experts_body, blocks), in_specs=[pl.Bloc...  24.8 us
    ppermute x14, waiting for transfers between devices, across(): return lax.ppermute(value, 'dp', other_side)  19.8 us
    ppermute x14, starting transfers between devices, up(): return lax.ppermute(value, 'dp', next_chip)  17.3 us
    ppermute x14, starting transfers between devices, across(): return lax.ppermute(value, 'dp', other_side)  16.7 us
    ppermute x14, waiting for transfers between devices, up(): return lax.ppermute(value, 'dp', next_chip)  11.8 us
    pallas_call x2, Pallas kernels, attend(): pl.pallas_call(functools.partial(attend_body, first), grid_spec=pltpu.Pre...  7.87 us
    pallas_call x2, Pallas kernels, dequant(): pl.pallas_call(dequant_body, grid=(steps,), in_specs=[smem, smem, smem, t...  6.91 us
    unnamed x44, local copies, waits for them, and re-layouts  5.22 us
  transfers between devices with their start and end apart: 34, of which 15 were waited for; matrix products, arithmetic and copies ran while one was open for 1% of the time, Pallas kernels for 34%

commit v1 on v0

v1 whole, which is shorter than its diff:
```python
import functools
import math

import jax
import jax.numpy as jnp
from jax import lax
from jax.experimental import pallas as pl
from jax.experimental.pallas import tpu as pltpu
from jax.sharding import PartitionSpec as P

HD = 128
QB = 128
BF16 = jnp.bfloat16
F32 = jnp.float32
TURN = jax.ShapeDtypeStruct((8, 128), jnp.int32)
ROUTE = 128
MIB = 1024 * 1024
LIGHT = pl.CostEstimate(flops=1, bytes_accessed=1, transcendentals=0)


def params(mib):
    return pltpu.CompilerParams(vmem_limit_bytes=mib * MIB)


def attend_body(
    first,
    count,
    _,
    lens_ref,
    tok_hbm,
    mask_ref,
    embed_ref,
    query_hbm,
    new_key_hbm,
    new_value_hbm,
    key_hbm,
    value_hbm,
    gain_ref,
    ids_ref,
    probs_ref,
    resid_ref,
    normed_ref,
    turn_ref,
    tok_ref,
    query_ref,
    new_key_ref,
    new_value_ref,
    key_ref,
    value_ref,
    sems,
):
    turn_ref[...] = jnp.zeros(TURN.shape, TURN.dtype)
    _, prefix, kv_width = key_ref.shape
    width = tok_ref.shape[1]
    block_len = tok_ref.shape[0] // count
    kv_heads = kv_width // HD
    group = width // HD // kv_heads
    scale = math.log2(math.e) / math.sqrt(HD)
    contract_last = (((1,), (1,)), ((), ()))

    copies = []
    for at in range(count):
        source = pl.ds((first + at) * block_len, block_len)
        rows = pl.ds(at * block_len, block_len)
        pairs = [
            (query_hbm.at[source], query_ref.at[rows]),
            (new_key_hbm.at[source], new_key_ref.at[rows]),
            (key_hbm.at[first + at], key_ref.at[at]),
            (new_value_hbm.at[source], new_value_ref.at[rows]),
            (value_hbm.at[first + at], value_ref.at[at]),
            (tok_hbm.at[source], tok_ref.at[rows]),
        ]
        copies.append(
            [pltpu.make_async_copy(a, b, sems.at[at, n]) for n, (a, b) in enumerate(pairs)]
        )
    for group_of in copies:
        for copy in group_of:
            copy.start()

    tok_rows = mask_ref.shape[0]
    probs = probs_ref[...]
    high_probs = probs.astype(BF16).astype(F32)
    top_k = ids_ref.shape[0]
    table_rows = jnp.concatenate(
        [
            ids_ref[...].astype(F32),
            high_probs,
            probs - high_probs,
            jnp.broadcast_to(mask_ref[...].reshape(1, tok_rows).astype(F32), (8, tok_rows)),
        ],
        axis=0,
    ).astype(BF16)
    all_rows = count * block_len
    row_at = lax.broadcasted_iota(jnp.int32, (all_rows, tok_rows), 0) + first * block_len
    on_row = row_at == lax.broadcasted_iota(jnp.int32, (all_rows, tok_rows), 1)
    table = lax.dot_general(
        on_row.astype(BF16), table_rows, contract_last, preferred_element_type=F32
    )
    lane = lax.broadcasted_iota(jnp.int32, (all_rows, ROUTE), 1)
    lane_id = (lane % (ROUTE // 2)).astype(F32)
    share = jnp.zeros((all_rows, ROUTE), F32)
    for k in range(top_k):
        high, low = (table[:, at + k : at + k + 1] for at in (top_k, 2 * top_k))
        share = share + jnp.where(
            lane_id == table[:, k : k + 1], jnp.where(lane < ROUTE // 2, high, low), 0.0
        )
    normed_ref[:, width:] = share.astype(BF16)
    mask = table[:, 3 * top_k : 3 * top_k + 1]
    embed = embed_ref[...].reshape(1, width).astype(F32)
    gain = gain_ref[...].reshape(1, width).astype(F32)

    for at in range(count):
        rows = slice(at * block_len, (at + 1) * block_len)
        length = lens_ref[first + at]
        for copy in copies[at][:5]:
            copy.wait()
        queries = [
            jnp.concatenate(
                [
                    query_ref[rows, g * HD : (g + 1) * HD]
                    for g in range(head * group, (head + 1) * group)
                ],
                axis=0,
            )
            for head in range(kv_heads)
        ]

        def over(live):
            position = lax.broadcasted_iota(jnp.int32, (1, live), 1)
            closed = jnp.where(position < length, 0.0, -1e30)
            for head in range(kv_heads):
                lanes = slice(head * HD, (head + 1) * HD)
                query = queries[head]
                far = lax.dot_general(
                    query, key_ref[at, :live, lanes], contract_last, preferred_element_type=F32
                )
                near = lax.dot_general(
                    query, new_key_ref[rows, lanes], contract_last, preferred_element_type=F32
                )
                far = far + closed
                top = jnp.maximum(
                    jnp.max(far, axis=1, keepdims=True), jnp.max(near, axis=1, keepdims=True)
                )
                far = jnp.exp2((far - top) * scale)
                near = jnp.exp2((near - top) * scale)
                total = jnp.sum(far, axis=1, keepdims=True) + jnp.sum(near, axis=1, keepdims=True)
                out = jnp.dot(
                    far.astype(BF16), value_ref[at, :live, lanes], preferred_element_type=F32
                )
                out = out + jnp.dot(
                    near.astype(BF16), new_value_ref[rows, lanes], preferred_element_type=F32
                )
                out = (out / total).astype(BF16).astype(F32)
                for g in range(group):
                    start = (head * group + g) * HD
                    resid_ref[rows, start : start + HD] = out[g * block_len : (g + 1) * block_len]

        chunk = min(256, prefix)
        chunks = prefix // chunk
        needed = lax.div(length + (chunk - 1), chunk)
        for number in range(1, chunks + 1):
            fits = needed <= number if number == 1 else needed == number
            pl.when(fits)(functools.partial(over, number * chunk))

        copies[at][5].wait()
        resid = resid_ref[rows] + jnp.where(mask[rows] > 0.5, embed, tok_ref[rows].astype(F32))
        mean_square = jnp.mean(resid * resid, axis=1, keepdims=True)
        resid_ref[rows] = resid
        normed_ref[rows, :width] = (resid * lax.rsqrt(mean_square + 1e-06) * gain).astype(BF16)


def attend(first, count, turn, lens, tokens, mask, embed, queries, new_keys, new_values, keys, values, gain, ids, probs):
    tok_rows, width = tokens.shape
    requests, prefix, kv_width = keys.shape
    rows = tok_rows // requests * count
    smem = pl.BlockSpec(memory_space=pltpu.SMEM)
    vmem = pl.BlockSpec(memory_space=pltpu.VMEM)
    hbm = pl.BlockSpec(memory_space=pltpu.HBM)
    return pl.pallas_call(
        functools.partial(attend_body, first, count),
        in_specs=[hbm, smem, hbm, vmem, vmem, hbm, hbm, hbm, hbm, hbm, vmem, vmem, vmem],
        out_specs=[vmem, vmem, vmem],
        out_shape=[
            jax.ShapeDtypeStruct((rows, width), F32),
            jax.ShapeDtypeStruct((rows, width + ROUTE), BF16),
            TURN,
        ],
        scratch_shapes=[
            pltpu.VMEM((rows, width), BF16),
            pltpu.VMEM((rows, width), BF16),
            pltpu.VMEM((rows, kv_width), BF16),
            pltpu.VMEM((rows, kv_width), BF16),
            pltpu.VMEM((count, prefix, kv_width), BF16),
            pltpu.VMEM((count, prefix, kv_width), BF16),
            pltpu.SemaphoreType.DMA((count, 6)),
        ],
        compiler_params=params(60 if first == 0 else 60),
        cost_estimate=pl.CostEstimate(
            flops=16 * rows * width * prefix,
            bytes_accessed=16 * count * prefix * kv_width + 48 * rows * width,
            transcendentals=rows * width // HD * prefix,
        ),
        name="attend",
    )(turn, lens, tokens, mask, embed, queries, new_keys, new_values, keys, values, gain, ids, probs)


def scale_blocks(factor_of, quant_ref, out_ref):
    row_count, col_count = quant_ref.shape[1:]
    first = pl.program_id(0) * (row_count // QB)
    for i in range(row_count // QB):
        factor = jnp.concatenate(
            [jnp.full((1, QB), factor_of(first + i, j), F32) for j in range(col_count // QB)],
            axis=1,
        )
        rows = pl.ds(pl.multiple_of((first + i) * QB, QB), QB)
        block = quant_ref[0, i * QB : (i + 1) * QB].astype(F32) * factor
        out_ref[rows] = block.astype(BF16)


def dequant_body(_, *refs):
    scales, quants, outs, turn_ref = refs[:2], refs[2:8], refs[8:12], refs[12]
    turn_ref[...] = jnp.zeros(TURN.shape, TURN.dtype)
    for own, scale in enumerate(scales):
        gate, up, down = quants[3 * own : 3 * own + 3]
        gate_up_out, down_out = outs[2 * own : 2 * own + 2]
        tall = scale.shape[1] // 3
        scale_blocks(lambda i, j, ref=scale: ref[0, j, i], gate, gate_up_out.at[0])
        scale_blocks(lambda i, j, ref=scale: ref[0, tall + j, i], up, gate_up_out.at[1])
        scale_blocks(lambda i, j, ref=scale: ref[0, 2 * tall + i, j], down, down_out)


def dequant(turn, own, other):
    _, width, hidden = own[0].shape
    steps = hidden // QB
    smem = pl.BlockSpec(memory_space=pltpu.SMEM)
    vmem = pl.BlockSpec(memory_space=pltpu.VMEM)
    tall = pl.BlockSpec((1, width // steps, hidden), lambda i: (0, i, 0))
    wide = pl.BlockSpec((1, hidden // steps, width), lambda i: (0, i, 0))
    gate_up = jax.ShapeDtypeStruct((2, width, hidden), BF16)
    down = jax.ShapeDtypeStruct((hidden, width), BF16)
    weights = pl.pallas_call(
        dequant_body,
        grid=(steps,),
        in_specs=[pl.BlockSpec(memory_space=pl.ANY)] + [smem] * 2 + [tall, tall, wide] * 2,
        out_specs=[vmem] * 5,
        out_shape=[gate_up, down] * 2 + [TURN],
        compiler_params=params(10),
        cost_estimate=LIGHT,
        name="dequant",
    )(turn, own[3], other[3], *own[:3], *other[:3])
    return weights[:2], weights[2:4], weights[4]


def experts_body(blocks, _, chip_ref, *refs):
    x_refs, refs = refs[:blocks], refs[blocks:]
    weight_refs, refs = refs[:4], refs[4:]
    out_refs, (turn_ref, x_all, total) = refs[:blocks], refs[blocks:]
    turn_ref[...] = jnp.zeros(TURN.shape, TURN.dtype)
    rows = x_refs[0].shape[0]
    width = x_all.shape[1]
    lane = lax.broadcasted_iota(jnp.int32, (rows, ROUTE), 1) % (ROUTE // 2)
    for at, ref in enumerate(x_refs):
        x_all[at * rows : (at + 1) * rows] = ref[:, :width]
    for number in range(2):
        gate_up, down = weight_refs[2 * number : 2 * number + 2]
        named = lane == chip_ref[number]
        shares = [jnp.where(named, ref[:, width:].astype(F32), 0.0) for ref in x_refs]
        share = jnp.sum(jnp.concatenate(shares, axis=0), axis=1, keepdims=True)
        hidden_width = down.shape[0]
        tile = min(256, hidden_width)
        for at in range(0, hidden_width, tile):
            cols = slice(at, at + tile)
            x = x_all[...]
            gate = jnp.dot(x, gate_up[0, :, cols], preferred_element_type=F32)
            up = jnp.dot(x, gate_up[1, :, cols], preferred_element_type=F32)
            hidden = (gate * jax.nn.sigmoid(gate) * up * share).astype(BF16)
            part = jnp.dot(hidden, down[cols, :], preferred_element_type=F32)
            if number == 0 and at == 0:
                total[...] = part
            else:
                total[...] += part
    for at, ref in enumerate(out_refs):
        ref[...] = total[at * rows : (at + 1) * rows].astype(BF16)


def experts(turn, xs, chip, own, other):
    rows = xs[0].shape[0]
    width = own[1].shape[1]
    hidden = own[1].shape[0]
    blocks = len(xs)
    all_rows = rows * blocks
    vmem = pl.BlockSpec(memory_space=pltpu.VMEM)
    return pl.pallas_call(
        functools.partial(experts_body, blocks),
        in_specs=[pl.BlockSpec(memory_space=pl.ANY), pl.BlockSpec(memory_space=pltpu.SMEM)]
        + [vmem] * (blocks + 4),
        out_specs=[vmem] * (blocks + 1),
        out_shape=[jax.ShapeDtypeStruct((rows, width), BF16)] * blocks + [TURN],
        scratch_shapes=[pltpu.VMEM((all_rows, width), BF16), pltpu.VMEM((all_rows, width), F32)],
        compiler_params=params(16),
        cost_estimate=LIGHT,
        name="experts",
    )(turn, chip, *xs, *own, *other)


def add(*terms):
    total = terms[0].astype(F32)
    for term in terms[1:]:
        total = total + term.astype(F32)
    return total.astype(BF16)


def shards(
    sizes,
    tokens,
    mask_positions,
    mask_embed,
    queries,
    new_keys,
    new_values,
    cache_keys,
    cache_values,
    prefix_lengths,
    expert_ids,
    gate_probs,
    norm_gain,
    gate_quant,
    gate_scale,
    up_quant,
    up_scale,
    down_quant,
    down_scale,
):
    depth, side = sizes
    devices = depth * side * 2
    tok_rows, width = tokens.shape
    requests = cache_keys.shape[0]
    me = lax.axis_index("dp")

    def place(z, y, core):
        return (z * side + y) * 2 + core

    everyone = [(a, b, c) for a in range(depth) for b in range(side) for c in range(2)]
    next_chip = [(place(a, b, c), place((a + 1) % depth, b, c)) for a, b, c in everyone]
    other_side = [(place(a, b, c), place(a, side - 1 - b, c)) for a, b, c in everyone]
    other_core = [(place(a, b, c), place(a, b, 1 - c)) for a, b, c in everyone]

    def up(value, name="sums"):
        with jax.named_scope(name + "_along_z"):
            return lax.ppermute(value, "dp", next_chip)

    def across(value, name):
        with jax.named_scope(name + "_along_y"):
            return lax.ppermute(value, "dp", other_side)

    scales = [jnp.swapaxes(gate_scale, 1, 2), jnp.swapaxes(up_scale, 1, 2), down_scale]
    quantized = (gate_quant, up_quant, down_quant, jnp.concatenate(scales, axis=1))
    from_core = [lax.ppermute(value, "dp", other_core) for value in quantized]
    chip = jnp.stack([me, me + 1 - 2 * (me % 2)])

    fixed = (
        prefix_lengths,
        tokens,
        mask_positions,
        mask_embed,
        queries,
        new_keys,
        new_values,
        cache_keys,
        cache_values,
        norm_gain,
        expert_ids.T,
        gate_probs.T,
    )
    turn = jnp.zeros(TURN.shape, TURN.dtype)
    if side == 1:
        resid, normed, turn = attend(0, requests, turn, *fixed)
        own, other, turn = dequant(turn, quantized, from_core)
        near, turn = experts(turn, [normed], chip, own, other)

        def step(_, carry):
            block, sums = carry
            block = up(block)
            part, _ = experts(turn, [block], chip, own, other)
            return block, add(up(sums), part)

        _, sums = lax.fori_loop(1, depth, step, (normed, jnp.zeros_like(near)))
        return (resid + near.astype(F32) + up(sums).astype(F32)).astype(BF16)

    halves = 2
    count = requests // halves
    last = halves - 1
    resids, rows_of, sides_of, parts, sums = {}, {}, {}, {}, {}

    def in_turn(values):
        nonlocal turn
        values, turn = lax.optimization_barrier((values, turn))
        return values

    def landed(*places):
        held = in_turn([where[key] for where, key in places])
        for (where, key), value in zip(places, held):
            where[key] = value

    def landed_part(back, half):
        parts[back, half] = in_turn(parts[back, half])

    def run_attend(half):
        nonlocal turn
        resids[half], rows_of[0, half], turn = attend(half * count, count, turn, *fixed)

    def send_on(back, half):
        rows = rows_of[back, half] = in_turn(rows_of[back, half])
        rows_of[back + 1, half] = up(rows, f"rows_{back + 1}_{half}")

    def send_across(back, half):
        if (back, half) == (depth - 1, last):
            rows = sides_of[back - 1, half] = in_turn(sides_of[back - 1, half])
            sides_of[back, half] = up(rows, f"side_{back}_{half}")
        else:
            rows = rows_of[back, half] = in_turn(rows_of[back, half])
            sides_of[back, half] = across(rows, f"rows_{back}_{half}")

    def run_experts(back, half):
        nonlocal turn
        here, there, turn = experts(
            turn, [rows_of[back, half], sides_of[back, half]], chip, own, other
        )
        parts[back, half] = here, there

    def send_part(back, half):
        here, there = parts[back, half]
        there = in_turn(there)
        if (back, half) == (1, last):
            sums["held"] = up(there, "held")
            parts[back, half] = [here]
        else:
            if (back, half) == (2, last):
                there = add(there, sums["held"])
            parts[back, half] = [here, across(there, f"part_{back}_{half}")]

    def send_sums(back, half):
        terms = list(parts[back, half])
        if back != 1:
            terms.append(sums[half])
        if back == 0:
            terms.append(resids[half])
        sums[half] = add(*in_turn(terms))
        if back != 0:
            sums[half] = up(sums[half], f"sums_{back}_{half}")

    a, b = 0, 1
    run_attend(a)
    send_on(0, a)
    send_across(0, a)
    run_attend(b)
    send_on(0, b)
    send_across(0, b)
    send_on(1, a)
    send_across(1, a)
    landed((sides_of, (0, a)))
    own, other, turn = dequant(turn, quantized, from_core)
    send_on(1, b)
    send_across(1, b)
    send_on(2, a)
    send_across(2, a)
    landed((sides_of, (0, b)))
    run_experts(1, a)
    send_part(1, a)
    send_on(2, b)
    send_across(2, b)
    run_experts(1, b)
    send_part(1, b)
    landed((rows_of, (3, a)))
    send_across(3, a)
    run_experts(2, a)
    send_part(2, a)
    send_sums(1, a)
    landed((rows_of, (3, b)), (sides_of, (2, b)), (sums, "held"))
    send_across(3, b)
    run_experts(2, b)
    send_part(2, b)
    send_sums(1, b)
    run_experts(3, a)
    send_part(3, a)
    landed_part(2, a)
    send_sums(2, a)
    run_experts(3, b)
    send_part(3, b)
    landed_part(2, b)
    send_sums(2, b)
    run_experts(0, a)
    send_part(0, a)
    landed_part(3, a)
    send_sums(3, a)
    run_experts(0, b)
    send_part(0, b)
    send_sums(3, b)
    send_sums(0, a)
    send_sums(0, b)
    return jnp.concatenate([sums[half] for half in range(halves)], 0)


def solution(mesh):
    in_specs = (
        P(("groups", "dp"), None),
        P(("groups", "dp")),
        P(),
        P(("groups", "dp"), None),
        P(("groups", "dp"), None),
        P(("groups", "dp"), None),
        P(("groups", "dp"), None, None),
        P(("groups", "dp"), None, None),
        P(("groups", "dp")),
        P(("groups", "dp"), None),
        P(("groups", "dp"), None),
        P(),
        P("dp", None, None),
        P("dp", None, None),
        P("dp", None, None),
        P("dp", None, None),
        P("dp", None, None),
        P("dp", None, None),
    )
    out_specs = P(("groups", "dp"), None)
    chips = mesh.shape["dp"] // 2
    sizes = (chips // 2, 2) if chips == 8 else (chips, 1)
    return jax.shard_map(
        functools.partial(shards, sizes),
        mesh=mesh,
        in_specs=in_specs,
        out_specs=out_specs,
        check_vma=False,
    )
```

time: 117 us -> 112 us (0.957)
  starting transfers between devices: 36.5 us -> 28 us
  waiting for transfers between devices: 32.4 us -> 35.5 us
    ppermute x14, waiting for transfers between devices: 11.8 us -> 33.5 us  [up(): return lax.ppermute(value, 'dp', next_chip)]
    ppermute x14, waiting for transfers between devices: 19.8 us -> 2.08 us  [across(): return lax.ppermute(value, 'dp', other_side)]
    ppermute x14, starting transfers between devices: 17.3 us -> 12.8 us  [up(): return lax.ppermute(value, 'dp', next_chip)]
    ppermute x14, starting transfers between devices: 16.7 us -> 14.2 us  [across(): return lax.ppermute(value, 'dp', other_side)]
    ppermute x6 -> x4, starting transfers between devices: 2.53 us -> 1.02 us  [shards(): from_core = [lax.ppermute(value, 'dp', other_core) for value in quantized]]
    unnamed x44 -> x16, local copies, waits for them, and re-layouts: 5.22 us -> 3.88 us
    pallas_call x4 -> x3, Pallas kernels: 14.8 us -> 16 us  [the longest x2 11.1 us: attend(): pl.pallas_call(functools.partial(attend_body, first, count), in_specs=[hb...]
  transfers between devices with their start and end apart: 34 -> 32, of which waited for: 15 -> 14; matrix products, arithmetic and copies ran while one was open for 1% -> 2% of each run, Pallas kernels for 34% -> 36%
where the time goes in v1:
time: 112 us; the launch traced here: 111 us
  Pallas kernels  40 us (36%)
  waiting for transfers between devices  35.5 us (32%)
  starting transfers between devices  28 us (25%)
  local copies, waits for them, and re-layouts  4.47 us (4%)
  other arithmetic  2.48 us (2%)
    ppermute x14, waiting for transfers between devices, up(): return lax.ppermute(value, 'dp', next_chip)  33.5 us
    pallas_call x8, Pallas kernels, experts(): pl.pallas_call(functools.partial(experts_body, blocks), in_specs=[pl.Bloc...  24 us
    ppermute x14, starting transfers between devices, across(): return lax.ppermute(value, 'dp', other_side)  14.2 us
    ppermute x14, starting transfers between devices, up(): return lax.ppermute(value, 'dp', next_chip)  12.8 us
    pallas_call x2, Pallas kernels, attend(): pl.pallas_call(functools.partial(attend_body, first, count), in_specs=[hb...  11.1 us
    pallas_call x1, Pallas kernels, dequant(): pl.pallas_call(dequant_body, grid=(steps,), in_specs=[pl.BlockSpec(memory...  4.87 us
    unnamed x16, local copies, waits for them, and re-layouts  3.88 us
  transfers between devices with their start and end apart: 32, of which 14 were waited for; matrix products, arithmetic and copies ran while one was open for 2% of the time, Pallas kernels for 36%

profile of v1, /device:TPU:0, one launch (start us, length us, event | category | flops | bytes accessed | tf_op | source)
XLA Modules:
  0.0 110.7 jit_solution(12446700534104939389)
XLA Ops:
  2.3 5.6 %attend.2 = (f32[64,2048]{1,0:T(8,128)}, bf16[64,2176]{1,0:T(8,128)(2,1)}, s32[8,128]{1,0:T(8,128)}) custom-call(s32[8,128]{1,0:T(8,128)} %broadcast_in_dim.3._, s32[4]{0:T(128)} %lens_ref.3, bf16[128,2048]{1,0:T(8,128)(2,1)} %tok_hbm.3, s32[128]{0:T(128)} %mask_ref.3, bf16[2048]{0:T(1024)(128)(2,1)} %embed_ref.3, bf16[128,2048]{1,0:T(8,128)(2,1)} %query_hbm.3, ...), custom_call_target="tpu_custom_call" | custom-call | flops 2147483648 | bytes 14680064 | tf_op jit(solution)/shard_map/attend/pallas_call | solution.py:179
  7.9 2.7 %collective-permute-start.2 = (bf16[64,2176]{1,0:T(8,128)(2,1)}, bf16[64,2176]{1,0:T(8,128)(2,1)S(1)}, u32[]{:S(2)}, u32[]{:S(2)}) collective-permute-start(bf16[64,2176]{1,0:T(8,128)(2,1)} %get-tuple-element.127.refs_0_), channel_id=1, source_target_pairs={{0,4},{1,5},{2,6},{3,7},{4,8},{5,9},{6,10},{7,11},{8,12},{9,13},{1... | collective-permute-start | bytes 835592 | tf_op jit(solution)/shard_map/rows_1_0_along_z/ppermute | solution.py:350
  12.1 5.5 %attend.3 = (f32[64,2048]{1,0:T(8,128)}, bf16[64,2176]{1,0:T(8,128)(2,1)}, s32[8,128]{1,0:T(8,128)}) custom-call(s32[8,128]{1,0:T(8,128)} %get-tuple-element.122._, s32[4]{0:T(128)} %lens_ref.3, bf16[128,2048]{1,0:T(8,128)(2,1)} %tok_hbm.3, s32[128]{0:T(128)} %mask_ref.3, bf16[2048]{0:T(1024)(128)(2,1)} %embed_ref.3, bf16[128,2048]{1,0:T(8,128)(2,1)} %query_hbm.3, ...), custom_call_target="tpu_custom_call" | custom-call | flops 2147483648 | bytes 14680064 | tf_op jit(solution)/shard_map/attend/pallas_call | solution.py:179
  17.7 1.8 %collective-permute-done.2.refs_0_ = bf16[64,2176]{1,0:T(8,128)(2,1)S(1)} collective-permute-done((bf16[64,2176]{1,0:T(8,128)(2,1)}, bf16[64,2176]{1,0:T(8,128)(2,1)S(1)}, u32[]{:S(2)}, u32[]{:S(2)}) %collective-permute-start.2) | collective-permute-done | bytes 278560 | tf_op jit(solution)/shard_map/rows_1_0_along_z/ppermute | solution.py:350
  27.1 4.9 %dequant.1 = (bf16[2,2048,512]{2,1,0:T(8,128)(2,1)S(1)}, bf16[512,2048]{1,0:T(8,128)(2,1)S(1)}, bf16[2,2048,512]{2,1,0:T(8,128)(2,1)S(1)}, bf16[512,2048]{1,0:T(8,128)(2,1)S(1)}, s32[8,128]{1,0:T(8,128)S(1)}) custom-call(s32[8,128]{1,0:T(8,128)S(1)} %copy-done.5, f32[1,12,16]{2,1,0:T(8,128)S(1)} %pad_maximum_fusion.1.refs_0_, ...), custom_call_target="tpu_custom_call" | custom-call | flops 1 | bytes 1 | tf_op jit(solution)/shard_map/dequant/pallas_call | solution.py:241
  32.0 3.5 %collective-permute-done.9.refs_0_ = bf16[64,2176]{1,0:T(8,128)(2,1)S(1)} collective-permute-done((bf16[64,2176]{1,0:T(8,128)(2,1)S(1)}, bf16[64,2176]{1,0:T(8,128)(2,1)S(1)}, u32[]{:S(2)}, u32[]{:S(2)}) %collective-permute-start.9) | collective-permute-done | bytes 278560 | tf_op jit(solution)/shard_map/rows_2_0_along_z/ppermute | solution.py:350
  37.6 3.3 %experts.8 = (bf16[64,2048]{1,0:T(8,128)(2,1)S(1)}, bf16[64,2048]{1,0:T(8,128)(2,1)S(1)}, s32[8,128]{1,0:T(8,128)S(1)}) custom-call(s32[8,128]{1,0:T(8,128)S(1)} %get-tuple-element.137._, s32[2]{0:T(128)S(1)} %pad_add_fusion.chip_ref, bf16[64,2176]{1,0:T(8,128)(2,1)S(1)} %collective-permute-done.2.refs_0_, bf16[64,2176]{1,0:T(8,128)(2,1)} %collective-permute-done.10.refs_1_, ...), custom_call_target="tpu_custom_call" | custom-call | flops 1 | bytes 1 | tf_op jit(solution)/shard_map/experts/pallas_call | solution.py:293
  40.9 1.9 %collective-permute-start.15 = (bf16[64,2048]{1,0:T(8,128)(2,1)S(1)}, bf16[64,2048]{1,0:T(8,128)(2,1)S(1)}, u32[]{:S(2)}, u32[]{:S(2)}) collective-permute-start(bf16[64,2048]{1,0:T(8,128)(2,1)S(1)} %get-tuple-element.154), channel_id=1, source_target_pairs={{0,2},{1,3},{2,0},{3,1},{4,6},{5,7},{6,4},{7,5},{8,10},{9,11},{10,... | collective-permute-start | bytes 786440 | tf_op jit(solution)/shard_map/part_1_0_along_y/ppermute | solution.py:354
  42.7 4.1 %collective-permute-done.7.refs_0_ = bf16[64,2176]{1,0:T(8,128)(2,1)S(1)} collective-permute-done((bf16[64,2176]{1,0:T(8,128)(2,1)S(1)}, bf16[64,2176]{1,0:T(8,128)(2,1)S(1)}, u32[]{:S(2)}, u32[]{:S(2)}) %collective-permute-start.7) | collective-permute-done | bytes 278560 | tf_op jit(solution)/shard_map/rows_2_1_along_z/ppermute | solution.py:350
  46.8 2.9 %experts.9 = (bf16[64,2048]{1,0:T(8,128)(2,1)S(1)}, bf16[64,2048]{1,0:T(8,128)(2,1)S(1)}, s32[8,128]{1,0:T(8,128)S(1)}) custom-call(s32[8,128]{1,0:T(8,128)S(1)} %get-tuple-element.148._, s32[2]{0:T(128)S(1)} %pad_add_fusion.chip_ref, bf16[64,2176]{1,0:T(8,128)(2,1)S(1)} %collective-permute-done.refs_0_, ...), custom_call_target="tpu_custom_call" | custom-call | flops 1 | bytes 1 | tf_op jit(solution)/shard_map/experts/pallas_call | solution.py:293
  51.0 2.8 %experts.10 = (bf16[64,2048]{1,0:T(8,128)(2,1)S(1)}, bf16[64,2048]{1,0:T(8,128)(2,1)S(1)}, s32[8,128]{1,0:T(8,128)S(1)}) custom-call(s32[8,128]{1,0:T(8,128)S(1)} %get-tuple-element.157._, s32[2]{0:T(128)S(1)} %pad_add_fusion.chip_ref, bf16[64,2176]{1,0:T(8,128)(2,1)S(1)} %collective-permute-done.9.refs_0_, ...), custom_call_target="tpu_custom_call" | custom-call | flops 1 | bytes 1 | tf_op jit(solution)/shard_map/experts/pallas_call | solution.py:293
  58.5 6.7 %collective-permute-done.14 = bf16[64,2048]{1,0:T(8,128)(2,1)S(1)} collective-permute-done((bf16[64,2048]{1,0:T(8,128)(2,1)S(1)}, bf16[64,2048]{1,0:T(8,128)(2,1)S(1)}, u32[]{:S(2)}, u32[]{:S(2)}) %collective-permute-start.14) | collective-permute-done | bytes 262176 | tf_op jit(solution)/shard_map/held_along_z/ppermute | solution.py:350
  65.2 6.0 %collective-permute-done.11.refs_0_ = bf16[64,2176]{1,0:T(8,128)(2,1)S(1)} collective-permute-done((bf16[64,2176]{1,0:T(8,128)(2,1)S(1)}, bf16[64,2176]{1,0:T(8,128)(2,1)S(1)}, u32[]{:S(2)}, u32[]{:S(2)}) %collective-permute-start.11) | collective-permute-done | bytes 278560 | tf_op jit(solution)/shard_map/rows_3_1_along_z/ppermute | solution.py:350
  71.2 2.9 %experts.11 = (bf16[64,2048]{1,0:T(8,128)(2,1)S(1)}, bf16[64,2048]{1,0:T(8,128)(2,1)S(1)}, s32[8,128]{1,0:T(8,128)S(1)}) custom-call(s32[8,128]{1,0:T(8,128)S(1)} %get-tuple-element.165._, s32[2]{0:T(128)S(1)} %pad_add_fusion.chip_ref, bf16[64,2176]{1,0:T(8,128)(2,1)S(1)} %collective-permute-done.7.refs_0_, ...), custom_call_target="tpu_custom_call" | custom-call | flops 1 | bytes 1 | tf_op jit(solution)/shard_map/experts/pallas_call | solution.py:293
  74.1 2.9 %experts.12 = (bf16[64,2048]{1,0:T(8,128)(2,1)S(1)}, bf16[64,2048]{1,0:T(8,128)(2,1)S(1)}, s32[8,128]{1,0:T(8,128)S(1)}) custom-call(s32[8,128]{1,0:T(8,128)S(1)} %get-tuple-element.176._, s32[2]{0:T(128)S(1)} %pad_add_fusion.chip_ref, bf16[64,2176]{1,0:T(8,128)(2,1)S(1)} %collective-permute-done.16.refs_0_, ...), custom_call_target="tpu_custom_call" | custom-call | flops 1 | bytes 1 | tf_op jit(solution)/shard_map/experts/pallas_call | solution.py:293
  79.8 2.5 %collective-permute-start.26 = (bf16[64,2048]{1,0:T(8,128)(2,1)S(1)}, bf16[64,2048]{1,0:T(8,128)(2,1)S(1)}, u32[]{:S(2)}, u32[]{:S(2)}) collective-permute-start(bf16[64,2048]{1,0:T(8,128)(2,1)S(1)} %add_convert_fusion.5), channel_id=1, source_target_pairs={{0,4},{1,5},{2,6},{3,7},{4,8},{5,9},{6,10},{7,11},{8,12},{9,13},{1... | collective-permute-start | bytes 786440 | tf_op jit(solution)/shard_map/sums_2_0_along_z/ppermute | solution.py:350
  82.8 2.9 %experts.13 = (bf16[64,2048]{1,0:T(8,128)(2,1)S(1)}, bf16[64,2048]{1,0:T(8,128)(2,1)S(1)}, s32[8,128]{1,0:T(8,128)S(1)}) custom-call(s32[8,128]{1,0:T(8,128)S(1)} %get-tuple-element.186._, s32[2]{0:T(128)S(1)} %pad_add_fusion.chip_ref, bf16[64,2176]{1,0:T(8,128)(2,1)S(1)} %collective-permute-done.11.refs_0_, ...), custom_call_target="tpu_custom_call" | custom-call | flops 1 | bytes 1 | tf_op jit(solution)/shard_map/experts/pallas_call | solution.py:293
  85.7 2.1 %collective-permute-done.23 = bf16[64,2048]{1,0:T(8,128)(2,1)S(1)} collective-permute-done((bf16[64,2048]{1,0:T(8,128)(2,1)S(1)}, bf16[64,2048]{1,0:T(8,128)(2,1)S(1)}, u32[]{:S(2)}, u32[]{:S(2)}) %collective-permute-start.23) | collective-permute-done | bytes 262176 | tf_op jit(solution)/shard_map/sums_1_1_along_z/ppermute | solution.py:350
  87.8 2.9 %experts.14 = (bf16[64,2048]{1,0:T(8,128)(2,1)S(1)}, bf16[64,2048]{1,0:T(8,128)(2,1)S(1)}, s32[8,128]{1,0:T(8,128)S(1)}) custom-call(s32[8,128]{1,0:T(8,128)S(1)} %get-tuple-element.195._, s32[2]{0:T(128)S(1)} %pad_add_fusion.chip_ref, bf16[64,2176]{1,0:T(8,128)(2,1)S(1)} %copy-done.4, bf16[64,2176]{1,0:T(8,128)(2,1)S(1)} %collective-permute-done.1.refs_1_, ...), custom_call_target="tpu_custom_call" | custom-call | flops 1 | bytes 1 | tf_op jit(solution)/shard_map/experts/pallas_call | solution.py:293
  91.9 2.1 %collective-permute-start.27 = (bf16[64,2048]{1,0:T(8,128)(2,1)S(1)}, bf16[64,2048]{1,0:T(8,128)(2,1)S(1)}, u32[]{:S(2)}, u32[]{:S(2)}) collective-permute-start(bf16[64,2048]{1,0:T(8,128)(2,1)S(1)} %add_convert_fusion.4), channel_id=1, source_target_pairs={{0,4},{1,5},{2,6},{3,7},{4,8},{5,9},{6,10},{7,11},{8,12},{9,13},{1... | collective-permute-start | bytes 786440 | tf_op jit(solution)/shard_map/sums_3_0_along_z/ppermute | solution.py:350
  94.7 3.4 %experts.15 = (bf16[64,2048]{1,0:T(8,128)(2,1)S(1)}, bf16[64,2048]{1,0:T(8,128)(2,1)S(1)}, s32[8,128]{1,0:T(8,128)}) custom-call(s32[8,128]{1,0:T(8,128)S(1)} %get-tuple-element.218._, s32[2]{0:T(128)S(1)} %pad_add_fusion.chip_ref, bf16[64,2176]{1,0:T(8,128)(2,1)S(1)} %copy-done.3, bf16[64,2176]{1,0:T(8,128)(2,1)S(1)} %collective-permute-done.8.refs_1_, ...), custom_call_target="tpu_custom_call" | custom-call | flops 1 | bytes 1 | tf_op jit(solution)/shard_map/experts/pallas_call | solution.py:293
  99.4 1.8 %collective-permute-done.30 = bf16[64,2048]{1,0:T(8,128)(2,1)S(1)} collective-permute-done((bf16[64,2048]{1,0:T(8,128)(2,1)S(1)}, bf16[64,2048]{1,0:T(8,128)(2,1)S(1)}, u32[]{:S(2)}, u32[]{:S(2)}) %collective-permute-start.30) | collective-permute-done | bytes 262176 | tf_op jit(solution)/shard_map/sums_2_1_along_z/ppermute | solution.py:350
  102.1 3.6 %collective-permute-done.27 = bf16[64,2048]{1,0:T(8,128)(2,1)S(1)} collective-permute-done((bf16[64,2048]{1,0:T(8,128)(2,1)S(1)}, bf16[64,2048]{1,0:T(8,128)(2,1)S(1)}, u32[]{:S(2)}, u32[]{:S(2)}) %collective-permute-start.27) | collective-permute-done | bytes 262176 | tf_op jit(solution)/shard_map/sums_3_0_along_z/ppermute | solution.py:350
  106.8 2.8 %collective-permute-done.31 = bf16[64,2048]{1,0:T(8,128)(2,1)S(1)} collective-permute-done((bf16[64,2048]{1,0:T(8,128)(2,1)S(1)}, bf16[64,2048]{1,0:T(8,128)(2,1)S(1)}, u32[]{:S(2)}, u32[]{:S(2)}) %collective-permute-start.31) | collective-permute-done | bytes 262176 | tf_op jit(solution)/shard_map/sums_3_1_along_z/ppermute | solution.py:350
  (78 shorter events, 28.9 us)
Async XLA Ops:
  0.0 21.2 %collective-permute-start.4 = (bf16[1,2048,512]{2,1,0:T(8,128)(2,1)}, bf16[1,2048,512]{2,1,0:T(8,128)(2,1)}, u32[]{:S(2)}, u32[]{:S(2)}) collective-permute-start(bf16[1,2048,512]{2,1,0:T(8,128)(2,1)} %refs_2_.1), channel_id=1, source_target_pairs={{0,1},{1,0},{2,3},{3,2},{4,5},{5,4},{6,7},{7,6},{8,9},{9,8},{10,11... | collective-permute-start | bytes 6291464 | tf_op jit(solution)/shard_map/ppermute | solution.py:358
  0.5 22.3 %collective-permute-start.5 = (bf16[1,2048,512]{2,1,0:T(8,128)(2,1)}, bf16[1,2048,512]{2,1,0:T(8,128)(2,1)}, u32[]{:S(2)}, u32[]{:S(2)}) collective-permute-start(bf16[1,2048,512]{2,1,0:T(8,128)(2,1)} %refs_3_.1), channel_id=1, source_target_pairs={{0,1},{1,0},{2,3},{3,2},{4,5},{5,4},{6,7},{7,6},{8,9},{9,8},{10,11... | collective-permute-start | bytes 6291464 | tf_op jit(solution)/shard_map/ppermute | solution.py:358
  0.5 22.7 %collective-permute-start.6 = (bf16[1,512,2048]{2,1,0:T(8,128)(2,1)}, bf16[1,512,2048]{2,1,0:T(8,128)(2,1)}, u32[]{:S(2)}, u32[]{:S(2)}) collective-permute-start(bf16[1,512,2048]{2,1,0:T(8,128)(2,1)} %refs_4_.1), channel_id=1, source_target_pairs={{0,1},{1,0},{2,3},{3,2},{4,5},{5,4},{6,7},{7,6},{8,9},{9,8},{10,11... | collective-permute-start | bytes 6291464 | tf_op jit(solution)/shard_map/ppermute | solution.py:358
  7.9 11.5 %collective-permute-start.2 = (bf16[64,2176]{1,0:T(8,128)(2,1)}, bf16[64,2176]{1,0:T(8,128)(2,1)S(1)}, u32[]{:S(2)}, u32[]{:S(2)}) collective-permute-start(bf16[64,2176]{1,0:T(8,128)(2,1)} %get-tuple-element.127.refs_0_), channel_id=1, source_target_pairs={{0,4},{1,5},{2,6},{3,7},{4,8},{5,9},{6,10},{7,11},{8,12},{9,13},{1... | collective-permute-start | bytes 835592 | tf_op jit(solution)/shard_map/rows_1_0_along_z/ppermute | solution.py:350
  19.4 12.5 %collective-permute-start = (bf16[64,2176]{1,0:T(8,128)(2,1)}, bf16[64,2176]{1,0:T(8,128)(2,1)S(1)}, u32[]{:S(2)}, u32[]{:S(2)}) collective-permute-start(bf16[64,2176]{1,0:T(8,128)(2,1)} %get-tuple-element.133.refs_0_), channel_id=1, source_target_pairs={{0,4},{1,5},{2,6},{3,7},{4,8},{5,9},{6,10},{7,11},{8,12},{9,13},{1... | collective-permute-start | bytes 835592 | tf_op jit(solution)/shard_map/rows_1_1_along_z/ppermute | solution.py:350
  19.4 16.0 %collective-permute-start.9 = (bf16[64,2176]{1,0:T(8,128)(2,1)S(1)}, bf16[64,2176]{1,0:T(8,128)(2,1)S(1)}, u32[]{:S(2)}, u32[]{:S(2)}) collective-permute-start(bf16[64,2176]{1,0:T(8,128)(2,1)S(1)} %collective-permute-done.2.refs_0_), channel_id=1, source_target_pairs={{0,4},{1,5},{2,6},{3,7},{4,8},{5,9},{6,10},{7,11},{8,12},{9,13},{1... | collective-permute-start | bytes 835592 | tf_op jit(solution)/shard_map/rows_2_0_along_z/ppermute | solution.py:350
  21.2 16.1 %collective-permute-start.8 = (bf16[64,2176]{1,0:T(8,128)(2,1)}, bf16[64,2176]{1,0:T(8,128)(2,1)S(1)}, u32[]{:S(2)}, u32[]{:S(2)}) collective-permute-start(bf16[64,2176]{1,0:T(8,128)(2,1)} %get-tuple-element.133.refs_0_), channel_id=1, source_target_pairs={{0,2},{1,3},{2,0},{3,1},{4,6},{5,7},{6,4},{7,5},{8,10},{9,11},{10,... | collective-permute-start | bytes 835592 | tf_op jit(solution)/shard_map/rows_0_1_along_y/ppermute | solution.py:354
  22.8 14.8 %collective-permute-start.10 = (bf16[64,2176]{1,0:T(8,128)(2,1)S(1)}, bf16[64,2176]{1,0:T(8,128)(2,1)}, u32[]{:S(2)}, u32[]{:S(2)}) collective-permute-start(bf16[64,2176]{1,0:T(8,128)(2,1)S(1)} %collective-permute-done.2.refs_0_), channel_id=1, source_target_pairs={{0,2},{1,3},{2,0},{3,1},{4,6},{5,7},{6,4},{7,5},{8,10},{9,11},{10,... | collective-permute-start | bytes 835592 | tf_op jit(solution)/shard_map/rows_1_0_along_y/ppermute | solution.py:354
  35.5 11.4 %collective-permute-start.7 = (bf16[64,2176]{1,0:T(8,128)(2,1)S(1)}, bf16[64,2176]{1,0:T(8,128)(2,1)S(1)}, u32[]{:S(2)}, u32[]{:S(2)}) collective-permute-start(bf16[64,2176]{1,0:T(8,128)(2,1)S(1)} %collective-permute-done.refs_0_), channel_id=1, source_target_pairs={{0,4},{1,5},{2,6},{3,7},{4,8},{5,9},{6,10},{7,11},{8,12},{9,13},{1... | collective-permute-start | bytes 835592 | tf_op jit(solution)/shard_map/rows_2_1_along_z/ppermute | solution.py:350
  35.5 11.4 %collective-permute-start.13 = (bf16[64,2176]{1,0:T(8,128)(2,1)S(1)}, bf16[64,2176]{1,0:T(8,128)(2,1)S(1)}, u32[]{:S(2)}, u32[]{:S(2)}) collective-permute-start(bf16[64,2176]{1,0:T(8,128)(2,1)S(1)} %collective-permute-done.refs_0_), channel_id=1, source_target_pairs={{0,2},{1,3},{2,0},{3,1},{4,6},{5,7},{6,4},{7,5},{8,10},{9,11},{10,... | collective-permute-start | bytes 835592 | tf_op jit(solution)/shard_map/rows_1_1_along_y/ppermute | solution.py:354
  36.2 14.1 %collective-permute-start.16 = (bf16[64,2176]{1,0:T(8,128)(2,1)S(1)}, bf16[64,2176]{1,0:T(8,128)(2,1)S(1)}, u32[]{:S(2)}, u32[]{:S(2)}) collective-permute-start(bf16[64,2176]{1,0:T(8,128)(2,1)S(1)} %collective-permute-done.9.refs_0_), channel_id=1, source_target_pairs={{0,4},{1,5},{2,6},{3,7},{4,8},{5,9},{6,10},{7,11},{8,12},{9,13},{1... | collective-permute-start | bytes 835592 | tf_op jit(solution)/shard_map/rows_3_0_along_z/ppermute | solution.py:350
  37.3 13.8 %collective-permute-start.17 = (bf16[64,2176]{1,0:T(8,128)(2,1)S(1)}, bf16[64,2176]{1,0:T(8,128)(2,1)S(1)}, u32[]{:S(2)}, u32[]{:S(2)}) collective-permute-start(bf16[64,2176]{1,0:T(8,128)(2,1)S(1)} %collective-permute-done.9.refs_0_), channel_id=1, source_target_pairs={{0,2},{1,3},{2,0},{3,1},{4,6},{5,7},{6,4},{7,5},{8,10},{9,11},{10,... | collective-permute-start | bytes 835592 | tf_op jit(solution)/shard_map/rows_2_0_along_y/ppermute | solution.py:354
  40.9 13.3 %collective-permute-start.15 = (bf16[64,2048]{1,0:T(8,128)(2,1)S(1)}, bf16[64,2048]{1,0:T(8,128)(2,1)S(1)}, u32[]{:S(2)}, u32[]{:S(2)}) collective-permute-start(bf16[64,2048]{1,0:T(8,128)(2,1)S(1)} %get-tuple-element.154), channel_id=1, source_target_pairs={{0,2},{1,3},{2,0},{3,1},{4,6},{5,7},{6,4},{7,5},{8,10},{9,11},{10,... | collective-permute-start | bytes 786440 | tf_op jit(solution)/shard_map/part_1_0_along_y/ppermute | solution.py:354
  54.2 11.0 %collective-permute-start.14 = (bf16[64,2048]{1,0:T(8,128)(2,1)S(1)}, bf16[64,2048]{1,0:T(8,128)(2,1)S(1)}, u32[]{:S(2)}, u32[]{:S(2)}) collective-permute-start(bf16[64,2048]{1,0:T(8,128)(2,1)S(1)} %get-tuple-element.152), channel_id=1, source_target_pairs={{0,4},{1,5},{2,6},{3,7},{4,8},{5,9},{6,10},{7,11},{8,12},{9,13},{1... | collective-permute-start | bytes 786440 | tf_op jit(solution)/shard_map/held_along_z/ppermute | solution.py:350
  54.4 16.8 %collective-permute-start.11 = (bf16[64,2176]{1,0:T(8,128)(2,1)S(1)}, bf16[64,2176]{1,0:T(8,128)(2,1)S(1)}, u32[]{:S(2)}, u32[]{:S(2)}) collective-permute-start(bf16[64,2176]{1,0:T(8,128)(2,1)S(1)} %collective-permute-done.7.refs_0_), channel_id=1, source_target_pairs={{0,4},{1,5},{2,6},{3,7},{4,8},{5,9},{6,10},{7,11},{8,12},{9,13},{1... | collective-permute-start | bytes 835592 | tf_op jit(solution)/shard_map/rows_3_1_along_z/ppermute | solution.py:350
  55.6 15.6 %collective-permute-start.12 = (bf16[64,2176]{1,0:T(8,128)(2,1)S(1)}, bf16[64,2176]{1,0:T(8,128)(2,1)S(1)}, u32[]{:S(2)}, u32[]{:S(2)}) collective-permute-start(bf16[64,2176]{1,0:T(8,128)(2,1)S(1)} %collective-permute-done.7.refs_0_), channel_id=1, source_target_pairs={{0,2},{1,3},{2,0},{3,1},{4,6},{5,7},{6,4},{7,5},{8,10},{9,11},{10,... | collective-permute-start | bytes 835592 | tf_op jit(solution)/shard_map/rows_2_1_along_y/ppermute | solution.py:354
  56.4 17.7 %collective-permute-start.20 = (bf16[64,2176]{1,0:T(8,128)(2,1)S(1)}, bf16[64,2176]{1,0:T(8,128)(2,1)S(1)}, u32[]{:S(2)}, u32[]{:S(2)}) collective-permute-start(bf16[64,2176]{1,0:T(8,128)(2,1)S(1)} %collective-permute-done.16.refs_0_), channel_id=1, source_target_pairs={{0,2},{1,3},{2,0},{3,1},{4,6},{5,7},{6,4},{7,5},{8,10},{9,11},{10,... | collective-permute-start | bytes 835592 | tf_op jit(solution)/shard_map/rows_3_0_along_y/ppermute | solution.py:354
  57.6 19.4 %collective-permute-start.19 = (bf16[64,2048]{1,0:T(8,128)(2,1)S(1)}, bf16[64,2048]{1,0:T(8,128)(2,1)S(1)}, u32[]{:S(2)}, u32[]{:S(2)}) collective-permute-start(bf16[64,2048]{1,0:T(8,128)(2,1)S(1)} %get-tuple-element.173), channel_id=1, source_target_pairs={{0,2},{1,3},{2,0},{3,1},{4,6},{5,7},{6,4},{7,5},{8,10},{9,11},{10,... | collective-permute-start | bytes 786440 | tf_op jit(solution)/shard_map/part_2_0_along_y/ppermute | solution.py:354
  65.2 11.8 %collective-permute-start.21 = (bf16[64,2048]{1,0:T(8,128)(2,1)S(1)}, bf16[64,2048]{1,0:T(8,128)(2,1)S(1)}, u32[]{:S(2)}, u32[]{:S(2)}) collective-permute-start(bf16[64,2048]{1,0:T(8,128)(2,1)S(1)} %add_convert_fusion.6), channel_id=1, source_target_pairs={{0,4},{1,5},{2,6},{3,7},{4,8},{5,9},{6,10},{7,11},{8,12},{9,13},{1... | collective-permute-start | bytes 786440 | tf_op jit(solution)/shard_map/sums_1_0_along_z/ppermute | solution.py:350
  71.2 11.6 %collective-permute-start.22 = (bf16[64,2176]{1,0:T(8,128)(2,1)S(1)}, bf16[64,2176]{1,0:T(8,128)(2,1)S(1)}, u32[]{:S(2)}, u32[]{:S(2)}) collective-permute-start(bf16[64,2176]{1,0:T(8,128)(2,1)S(1)} %collective-permute-done.12.refs_1_), channel_id=1, source_target_pairs={{0,4},{1,5},{2,6},{3,7},{4,8},{5,9},{6,10},{7,11},{8,12},{9,13},{1... | collective-permute-start | bytes 835592 | tf_op jit(solution)/shard_map/side_3_1_along_z/ppermute | solution.py:350
  78.0 12.8 %collective-permute-start.25 = (bf16[64,2048]{1,0:T(8,128)(2,1)S(1)}, bf16[64,2048]{1,0:T(8,128)(2,1)S(1)}, u32[]{:S(2)}, u32[]{:S(2)}) collective-permute-start(bf16[64,2048]{1,0:T(8,128)(2,1)S(1)} %get-tuple-element.202), channel_id=1, source_target_pairs={{0,2},{1,3},{2,0},{3,1},{4,6},{5,7},{6,4},{7,5},{8,10},{9,11},{10,... | collective-permute-start | bytes 786440 | tf_op jit(solution)/shard_map/part_3_0_along_y/ppermute | solution.py:354
  79.8 11.0 %collective-permute-start.26 = (bf16[64,2048]{1,0:T(8,128)(2,1)S(1)}, bf16[64,2048]{1,0:T(8,128)(2,1)S(1)}, u32[]{:S(2)}, u32[]{:S(2)}) collective-permute-start(bf16[64,2048]{1,0:T(8,128)(2,1)S(1)} %add_convert_fusion.5), channel_id=1, source_target_pairs={{0,4},{1,5},{2,6},{3,7},{4,8},{5,9},{6,10},{7,11},{8,12},{9,13},{1... | collective-permute-start | bytes 786440 | tf_op jit(solution)/shard_map/sums_2_0_along_z/ppermute | solution.py:350
  91.9 13.8 %collective-permute-start.27 = (bf16[64,2048]{1,0:T(8,128)(2,1)S(1)}, bf16[64,2048]{1,0:T(8,128)(2,1)S(1)}, u32[]{:S(2)}, u32[]{:S(2)}) collective-permute-start(bf16[64,2048]{1,0:T(8,128)(2,1)S(1)} %add_convert_fusion.4), channel_id=1, source_target_pairs={{0,4},{1,5},{2,6},{3,7},{4,8},{5,9},{6,10},{7,11},{8,12},{9,13},{1... | collective-permute-start | bytes 786440 | tf_op jit(solution)/shard_map/sums_3_0_along_z/ppermute | solution.py:350
  94.0 11.7 %collective-permute-start.24 = (bf16[64,2048]{1,0:T(8,128)(2,1)S(1)}, bf16[64,2048]{1,0:T(8,128)(2,1)S(1)}, u32[]{:S(2)}, u32[]{:S(2)}) collective-permute-start(bf16[64,2048]{1,0:T(8,128)(2,1)S(1)} %get-tuple-element.200), channel_id=1, source_target_pairs={{0,2},{1,3},{2,0},{3,1},{4,6},{5,7},{6,4},{7,5},{8,10},{9,11},{10,... | collective-permute-start | bytes 786440 | tf_op jit(solution)/shard_map/part_0_0_along_y/ppermute | solution.py:354
  (16 other events, 140.8 us)

commit v2 on v1

--- a/solution.py
+++ b/solution.py
@@ -194,7 +194,7 @@
             pltpu.VMEM((count, prefix, kv_width), BF16),
             pltpu.SemaphoreType.DMA((count, 6)),
         ],
-        compiler_params=params(60 if first == 0 else 60),
+        compiler_params=params(60),
         cost_estimate=pl.CostEstimate(
             flops=16 * rows * width * prefix,
             bytes_accessed=16 * count * prefix * kv_width + 48 * rows * width,
@@ -355,7 +355,6 @@
 
     scales = [jnp.swapaxes(gate_scale, 1, 2), jnp.swapaxes(up_scale, 1, 2), down_scale]
     quantized = (gate_quant, up_quant, down_quant, jnp.concatenate(scales, axis=1))
-    from_core = [lax.ppermute(value, "dp", other_core) for value in quantized]
     chip = jnp.stack([me, me + 1 - 2 * (me % 2)])
 
     fixed = (
@@ -372,9 +371,10 @@
         expert_ids.T,
         gate_probs.T,
     )
-    turn = jnp.zeros(TURN.shape, TURN.dtype)
+    turn = expert_ids.T
     if side == 1:
         resid, normed, turn = attend(0, requests, turn, *fixed)
+        from_core = [lax.ppermute(value, "dp", other_core) for value in quantized]
         own, other, turn = dequant(turn, quantized, from_core)
         near, turn = experts(turn, [normed], chip, own, other)
 
@@ -390,115 +390,143 @@
     halves = 2
     count = requests // halves
     last = halves - 1
-    resids, rows_of, sides_of, parts, sums = {}, {}, {}, {}, {}
+    here, resids, totals = {}, {}, {}
 
     def in_turn(values):
         nonlocal turn
         values, turn = lax.optimization_barrier((values, turn))
         return values
 
-    def landed(*places):
-        held = in_turn([where[key] for where, key in places])
-        for (where, key), value in zip(places, held):
-            where[key] = value
-
-    def landed_part(back, half):
-        parts[back, half] = in_turn(parts[back, half])
+    from_core = [None] * len(quantized)
+
+    def swap(number):
+        from_core[number] = lax.ppermute(in_turn(quantized[number]), "dp", other_core)
+
+    def swapped(number):
+        from_core[number] = in_turn(from_core[number])
 
     def run_attend(half):
         nonlocal turn
-        resids[half], rows_of[0, half], turn = attend(half * count, count, turn, *fixed)
-
-    def send_on(back, half):
-        rows = rows_of[back, half] = in_turn(rows_of[back, half])
-        rows_of[back + 1, half] = up(rows, f"rows_{back + 1}_{half}")
-
-    def send_across(back, half):
-        if (back, half) == (depth - 1, last):
-            rows = sides_of[back - 1, half] = in_turn(sides_of[back - 1, half])
-            sides_of[back, half] = up(rows, f"side_{back}_{half}")
-        else:
-            rows = rows_of[back, half] = in_turn(rows_of[back, half])
-            sides_of[back, half] = across(rows, f"rows_{back}_{half}")
-
-    def run_experts(back, half):
+        resids[half], here["z", 0, half], turn = attend(half * count, count, turn, *fixed)
+
+    def start(kind, slot, half):
+        key = (kind, slot, half)
+        route, source = across, key
+        if kind == "z":
+            route, source = up, ("z", slot - 1, half)
+        elif kind == "c":
+            route = up
+        elif key == ("y", depth - 1, last):
+            route, source = up, ("y", slot - 1, half)
+        elif kind == "y":
+            source = ("z", slot, half)
+        elif key == ("r", 1, last):
+            route = up
+        here[key] = route(in_turn(totals[key] if kind in "rc" else here[source]), f"{kind}{slot}_{half}")
+
+    def land(kind, slot, half):
+        key = (kind, slot, half)
+        here[key] = in_turn(here[key])
+
+    def run_experts(slot, half):
         nonlocal turn
-        here, there, turn = experts(
-            turn, [rows_of[back, half], sides_of[back, half]], chip, own, other
+        mine, totals["r", slot, half], turn = experts(
+            turn, [here["z", slot, half], here["y", slot, half]], chip, own, other
         )
-        parts[back, half] = here, there
-
-    def send_part(back, half):
-        here, there = parts[back, half]
-        there = in_turn(there)
-        if (back, half) == (1, last):
-            sums["held"] = up(there, "held")
-            parts[back, half] = [here]
-        else:
-            if (back, half) == (2, last):
-                there = add(there, sums["held"])
-            parts[back, half] = [here, across(there, f"part_{back}_{half}")]
-
-    def send_sums(back, half):
-        terms = list(parts[back, half])
-        if back != 1:
-            terms.append(sums[half])
-        if back == 0:
+        totals["e", slot, half] = mine
+
+    def run_add(slot, half):
+        terms = [totals["e", slot, half]]
+        if (slot, half) != (1, last):
+            terms.append(here["r", slot, half])
+        if slot != 1:
+            terms.append(here["c", slot - 1 if slot else depth - 1, half])
+        if slot == 0:
             terms.append(resids[half])
-        sums[half] = add(*in_turn(terms))
-        if back != 0:
-            sums[half] = up(sums[half], f"sums_{back}_{half}")
+        totals["c", slot, half] = add(*in_turn(terms))
+
+    def run_held():
+        terms = [totals["r", 2, last], here["r", 1, last]]
+        totals["r", 2, last] = add(*in_turn(terms))
 
     a, b = 0, 1
+    swap(0)
+    swap(1)
+    swap(2)
     run_attend(a)
-    send_on(0, a)
-    send_across(0, a)
+    start("z", 1, a)
+    start("y", 0, a)
+    swap(3)
     run_attend(b)
-    send_on(0, b)
-    send_across(0, b)
-    send_on(1, a)
-    send_across(1, a)
-    landed((sides_of, (0, a)))
+    start("z", 1, b)
+    swapped(2)
+    start("y", 0, b)
+    land("z", 1, a)
+    swapped(3)
+    start("z", 2, a)
+    start("y", 1, a)
+    land("y", 0, a)
     own, other, turn = dequant(turn, quantized, from_core)
-    send_on(1, b)
-    send_across(1, b)
-    send_on(2, a)
-    send_across(2, a)
-    landed((sides_of, (0, b)))
+    start("z", 2, b)
+    start("y", 1, b)
+    land("y", 0, b)
+    land("z", 2, a)
+    land("y", 1, a)
+    start("z", 3, a)
+    start("y", 2, a)
     run_experts(1, a)
-    send_part(1, a)
-    send_on(2, b)
-    send_across(2, b)
+    start("r", 1, a)
+    land("z", 2, b)
+    start("z", 3, b)
+    start("y", 2, b)
+    land("y", 1, b)
     run_experts(1, b)
-    send_part(1, b)
-    landed((rows_of, (3, a)))
-    send_across(3, a)
+    start("r", 1, b)
+    land("z", 3, a)
+    land("y", 2, a)
+    start("y", 3, a)
     run_experts(2, a)
-    send_part(2, a)
-    send_sums(1, a)
-    landed((rows_of, (3, b)), (sides_of, (2, b)), (sums, "held"))
-    send_across(3, b)
+    run_add(1, b)
+    start("r", 2, a)
+    land("r", 1, a)
+    run_add(1, a)
+    start("c", 1, a)
+    land("z", 3, b)
+    land("y", 2, b)
+    start("y", 3, b)
     run_experts(2, b)
-    send_part(2, b)
-    send_sums(1, b)
+    land("r", 1, b)
+    land("y", 3, a)
+    run_held()
+    land("r", 2, a)
+    start("r", 2, b)
+    start("c", 1, b)
     run_experts(3, a)
-    send_part(3, a)
-    landed_part(2, a)
-    send_sums(2, a)
+    start("r", 3, a)
+    run_add(2, a)
+    start("c", 2, a)
     run_experts(3, b)
-    send_part(3, b)
-    landed_part(2, b)
-    send_sums(2, b)
+    start("r", 3, b)
+    land("c", 1, b)
+    land("r", 2, b)
+    run_add(2, b)
+    start("c", 2, b)
     run_experts(0, a)
-    send_part(0, a)
-    landed_part(3, a)
-    send_sums(3, a)
+    land("c", 2, a)
+    land("r", 3, a)
+    run_add(3, a)
+    start("c", 3, a)
     run_experts(0, b)
-    send_part(0, b)
-    send_sums(3, b)
-    send_sums(0, a)
-    send_sums(0, b)
-    return jnp.concatenate([sums[half] for half in range(halves)], 0)
+    start("r", 0, b)
+    start("r", 0, a)
+    land("c", 2, b)
+    land("r", 3, b)
+    run_add(3, b)
+    run_add(0, a)
+    land("r", 0, b)
+    start("c", 3, b)
+    run_add(0, b)
+    return jnp.concatenate([totals["c", 0, half] for half in range(halves)], 0)
 
 
 def solution(mesh):

time: 112 us -> 107 us (0.955)
  waiting for transfers between devices: 35.5 us -> 26.1 us
  starting transfers between devices: 28 us -> 35.4 us
    ppermute x14, waiting for transfers between devices: 33.5 us -> 14 us  [up(): return lax.ppermute(value, 'dp', next_chip)]
    ppermute x14, waiting for transfers between devices: 2.08 us -> 12.1 us  [across(): return lax.ppermute(value, 'dp', other_side)]
    ppermute x14, starting transfers between devices: 12.8 us -> 16.3 us  [up(): return lax.ppermute(value, 'dp', next_chip)]
    ppermute x14, starting transfers between devices: 14.2 us -> 16.8 us  [across(): return lax.ppermute(value, 'dp', other_side)]
    ppermute x4, starting transfers between devices: 1.02 us -> 2.26 us  [swap(): lax.ppermute(in_turn(quantized[number]), 'dp', other_core)]
    unnamed x16 -> x22, local copies, waits for them, and re-layouts: 3.88 us -> 3.89 us
  transfers between devices with their start and end apart: 32 -> 32, of which waited for: 14 -> 15; matrix products, arithmetic and copies ran while one was open for 2% -> 1% of each run, Pallas kernels for 36% -> 37%
where the time goes in v2:
time: 107 us; the launch traced here: 106 us
  Pallas kernels  39 us (36%)
  starting transfers between devices  35.4 us (33%)
  waiting for transfers between devices  26.1 us (24%)
  local copies, waits for them, and re-layouts  3.89 us (4%)
  other arithmetic  1.76 us (2%)
    pallas_call x8, Pallas kernels, experts(): pl.pallas_call(functools.partial(experts_body, blocks), in_specs=[pl.Bloc...  24 us
    ppermute x14, starting transfers between devices, across(): return lax.ppermute(value, 'dp', other_side)  16.8 us
    ppermute x14, starting transfers between devices, up(): return lax.ppermute(value, 'dp', next_chip)  16.3 us
    ppermute x14, waiting for transfers between devices, up(): return lax.ppermute(value, 'dp', next_chip)  14 us
    ppermute x14, waiting for transfers between devices, across(): return lax.ppermute(value, 'dp', other_side)  12.1 us
    pallas_call x2, Pallas kernels, attend(): pl.pallas_call(functools.partial(attend_body, first, count), in_specs=[hb...  10.2 us
    pallas_call x1, Pallas kernels, dequant(): pl.pallas_call(dequant_body, grid=(steps,), in_specs=[pl.BlockSpec(memory...  4.87 us
    unnamed x22, local copies, waits for them, and re-layouts  3.89 us
  transfers between devices with their start and end apart: 32, of which 15 were waited for; matrix products, arithmetic and copies ran while one was open for 1% of the time, Pallas kernels for 37%

profile of v2, /device:TPU:0, one launch (start us, length us, event | category | flops | bytes accessed | tf_op | source)
XLA Modules:
  0.0 106.3 jit_solution(18193097472920491903)
XLA Ops:
  1.0 5.2 %attend.2 = (f32[64,2048]{1,0:T(8,128)}, bf16[64,2176]{1,0:T(8,128)(2,1)}, s32[8,128]{1,0:T(8,128)}) custom-call(s32[8,128]{1,0:T(8,128)} %bitcast.8, s32[4]{0:T(128)} %lens_ref.3, bf16[128,2048]{1,0:T(8,128)(2,1)} %tok_hbm.3, s32[128]{0:T(128)} %mask_ref.3, bf16[2048]{0:T(1024)(128)(2,1)} %embed_ref.3, bf16[128,2048]{1,0:T(8,128)(2,1)} %query_hbm.3, ...), custom_call_target="tpu_custom_call" | custom-call | flops 2147483648 | bytes 14680064 | tf_op jit(solution)/shard_map/attend/pallas_call | solution.py:179
  6.2 2.4 %collective-permute-start.2 = (bf16[64,2176]{1,0:T(8,128)(2,1)}, bf16[64,2176]{1,0:T(8,128)(2,1)S(1)}, u32[]{:S(2)}, u32[]{:S(2)}) collective-permute-start(bf16[64,2176]{1,0:T(8,128)(2,1)} %get-tuple-element.180.refs_0_), channel_id=1, source_target_pairs={{0,4},{1,5},{2,6},{3,7},{4,8},{5,9},{6,10},{7,11},{8,12},{9,13},{1... | collective-permute-start | bytes 835592 | tf_op jit(solution)/shard_map/z1_0_along_z/ppermute | solution.py:350
  10.1 5.0 %attend.3 = (f32[64,2048]{1,0:T(8,128)}, bf16[64,2176]{1,0:T(8,128)(2,1)}, s32[8,128]{1,0:T(8,128)}) custom-call(s32[8,128]{1,0:T(8,128)} %get-tuple-element.175._, s32[4]{0:T(128)} %lens_ref.3, bf16[128,2048]{1,0:T(8,128)(2,1)} %tok_hbm.3, s32[128]{0:T(128)} %mask_ref.3, bf16[2048]{0:T(1024)(128)(2,1)} %embed_ref.3, bf16[128,2048]{1,0:T(8,128)(2,1)} %query_hbm.3, ...), custom_call_target="tpu_custom_call" | custom-call | flops 2147483648 | bytes 14680064 | tf_op jit(solution)/shard_map/attend/pallas_call | solution.py:179
  17.9 1.9 %collective-permute-start.9 = (bf16[64,2176]{1,0:T(8,128)(2,1)}, bf16[64,2176]{1,0:T(8,128)(2,1)S(1)}, u32[]{:S(2)}, u32[]{:S(2)}) collective-permute-start(bf16[64,2176]{1,0:T(8,128)(2,1)} %get-tuple-element.199.refs_0_), channel_id=1, source_target_pairs={{0,2},{1,3},{2,0},{3,1},{4,6},{5,7},{6,4},{7,5},{8,10},{9,11},{10,... | collective-permute-start | bytes 835592 | tf_op jit(solution)/shard_map/y0_1_along_y/ppermute | solution.py:354
  25.0 4.9 %dequant.1 = (bf16[2,2048,512]{2,1,0:T(8,128)(2,1)S(1)}, bf16[512,2048]{1,0:T(8,128)(2,1)S(1)}, bf16[2,2048,512]{2,1,0:T(8,128)(2,1)S(1)}, bf16[512,2048]{1,0:T(8,128)(2,1)S(1)}, s32[8,128]{1,0:T(8,128)S(1)}) custom-call(s32[8,128]{1,0:T(8,128)S(1)} %copy-done.5, f32[1,12,16]{2,1,0:T(8,128)S(1)} %pad_maximum_fusion.1.refs_0_, ...), custom_call_target="tpu_custom_call" | custom-call | flops 1 | bytes 1 | tf_op jit(solution)/shard_map/dequant/pallas_call | solution.py:241
  33.1 1.8 %collective-permute-done.8.refs_0_ = bf16[64,2176]{1,0:T(8,128)(2,1)S(1)} collective-permute-done((bf16[64,2176]{1,0:T(8,128)(2,1)S(1)}, bf16[64,2176]{1,0:T(8,128)(2,1)S(1)}, u32[]{:S(2)}, u32[]{:S(2)}) %collective-permute-start.8) | collective-permute-done | bytes 278560 | tf_op jit(solution)/shard_map/z2_0_along_z/ppermute | solution.py:350
  36.7 3.3 %experts.8 = (bf16[64,2048]{1,0:T(8,128)(2,1)S(1)}, bf16[64,2048]{1,0:T(8,128)(2,1)S(1)}, s32[8,128]{1,0:T(8,128)S(1)}) custom-call(s32[8,128]{1,0:T(8,128)S(1)} %get-tuple-element.208._, s32[2]{0:T(128)S(1)} %pad_add_fusion.chip_ref, bf16[64,2176]{1,0:T(8,128)(2,1)S(1)} %collective-permute-done.2.refs_0_, bf16[64,2176]{1,0:T(8,128)(2,1)} %collective-permute-done.10.refs_1_, ...), custom_call_target="tpu_custom_call" | custom-call | flops 1 | bytes 1 | tf_op jit(solution)/shard_map/experts/pallas_call | solution.py:293
  41.4 2.8 %experts.9 = (bf16[64,2048]{1,0:T(8,128)(2,1)S(1)}, bf16[64,2048]{1,0:T(8,128)(2,1)S(1)}, s32[8,128]{1,0:T(8,128)S(1)}) custom-call(s32[8,128]{1,0:T(8,128)S(1)} %get-tuple-element.226._, s32[2]{0:T(128)S(1)} %pad_add_fusion.chip_ref, bf16[64,2176]{1,0:T(8,128)(2,1)S(1)} %collective-permute-done.refs_0_, ...), custom_call_target="tpu_custom_call" | custom-call | flops 1 | bytes 1 | tf_op jit(solution)/shard_map/experts/pallas_call | solution.py:293
  44.2 1.9 %collective-permute-start.12 = (bf16[64,2176]{1,0:T(8,128)(2,1)S(1)}, bf16[64,2176]{1,0:T(8,128)(2,1)S(1)}, u32[]{:S(2)}, u32[]{:S(2)}) collective-permute-start(bf16[64,2176]{1,0:T(8,128)(2,1)S(1)} %collective-permute-done.7.refs_0_), channel_id=1, source_target_pairs={{0,4},{1,5},{2,6},{3,7},{4,8},{5,9},{6,10},{7,11},{8,12},{9,13},{1... | collective-permute-start | bytes 835592 | tf_op jit(solution)/shard_map/z3_1_along_z/ppermute | solution.py:350
  48.1 2.8 %experts.10 = (bf16[64,2048]{1,0:T(8,128)(2,1)S(1)}, bf16[64,2048]{1,0:T(8,128)(2,1)S(1)}, s32[8,128]{1,0:T(8,128)S(1)}) custom-call(s32[8,128]{1,0:T(8,128)S(1)} %get-tuple-element.235._, s32[2]{0:T(128)S(1)} %pad_add_fusion.chip_ref, bf16[64,2176]{1,0:T(8,128)(2,1)S(1)} %collective-permute-done.8.refs_0_, ...), custom_call_target="tpu_custom_call" | custom-call | flops 1 | bytes 1 | tf_op jit(solution)/shard_map/experts/pallas_call | solution.py:293
  50.9 1.8 %collective-permute-done.13 = bf16[64,2048]{1,0:T(8,128)(2,1)S(1)} collective-permute-done((bf16[64,2048]{1,0:T(8,128)(2,1)S(1)}, bf16[64,2048]{1,0:T(8,128)(2,1)S(1)}, u32[]{:S(2)}, u32[]{:S(2)}) %collective-permute-start.13) | collective-permute-done | bytes 262176 | tf_op jit(solution)/shard_map/r1_0_along_y/ppermute | solution.py:354
  55.1 3.6 %collective-permute-done.11.refs_1_ = bf16[64,2176]{1,0:T(8,128)(2,1)S(1)} collective-permute-done((bf16[64,2176]{1,0:T(8,128)(2,1)S(1)}, bf16[64,2176]{1,0:T(8,128)(2,1)S(1)}, u32[]{:S(2)}, u32[]{:S(2)}) %collective-permute-start.11) | collective-permute-done | bytes 278560 | tf_op jit(solution)/shard_map/y2_1_along_y/ppermute | solution.py:354
  58.7 2.9 %experts.11 = (bf16[64,2048]{1,0:T(8,128)(2,1)S(1)}, bf16[64,2048]{1,0:T(8,128)(2,1)S(1)}, s32[8,128]{1,0:T(8,128)S(1)}) custom-call(s32[8,128]{1,0:T(8,128)S(1)} %get-tuple-element.249._, s32[2]{0:T(128)S(1)} %pad_add_fusion.chip_ref, bf16[64,2176]{1,0:T(8,128)(2,1)S(1)} %collective-permute-done.7.refs_0_, ...), custom_call_target="tpu_custom_call" | custom-call | flops 1 | bytes 1 | tf_op jit(solution)/shard_map/experts/pallas_call | solution.py:293
  61.6 2.1 %collective-permute-start.22 = (bf16[64,2048]{1,0:T(8,128)(2,1)S(1)}, bf16[64,2048]{1,0:T(8,128)(2,1)S(1)}, u32[]{:S(2)}, u32[]{:S(2)}) collective-permute-start(bf16[64,2048]{1,0:T(8,128)(2,1)S(1)} %add_convert_fusion.7), channel_id=1, source_target_pairs={{0,4},{1,5},{2,6},{3,7},{4,8},{5,9},{6,10},{7,11},{8,12},{9,13},{1... | collective-permute-start | bytes 786440 | tf_op jit(solution)/shard_map/c1_0_along_z/ppermute | solution.py:350
  64.7 3.1 %collective-permute-done.19 = bf16[64,2048]{1,0:T(8,128)(2,1)S(1)} collective-permute-done((bf16[64,2048]{1,0:T(8,128)(2,1)S(1)}, bf16[64,2048]{1,0:T(8,128)(2,1)S(1)}, u32[]{:S(2)}, u32[]{:S(2)}) %collective-permute-start.19) | collective-permute-done | bytes 262176 | tf_op jit(solution)/shard_map/r2_0_along_y/ppermute | solution.py:354
  67.9 2.9 %experts.12 = (bf16[64,2048]{1,0:T(8,128)(2,1)S(1)}, bf16[64,2048]{1,0:T(8,128)(2,1)S(1)}, s32[8,128]{1,0:T(8,128)S(1)}) custom-call(s32[8,128]{1,0:T(8,128)S(1)} %get-tuple-element.271._, s32[2]{0:T(128)S(1)} %pad_add_fusion.chip_ref, bf16[64,2176]{1,0:T(8,128)(2,1)S(1)} %collective-permute-done.14.refs_0_, ...), custom_call_target="tpu_custom_call" | custom-call | flops 1 | bytes 1 | tf_op jit(solution)/shard_map/experts/pallas_call | solution.py:293
  70.8 2.0 %collective-permute-start.21 = (bf16[64,2048]{1,0:T(8,128)(2,1)S(1)}, bf16[64,2048]{1,0:T(8,128)(2,1)S(1)}, u32[]{:S(2)}, u32[]{:S(2)}) collective-permute-start(bf16[64,2048]{1,0:T(8,128)(2,1)S(1)} %get-tuple-element.267), channel_id=1, source_target_pairs={{0,4},{1,5},{2,6},{3,7},{4,8},{5,9},{6,10},{7,11},{8,12},{9,13},{1... | collective-permute-start | bytes 786440 | tf_op jit(solution)/shard_map/c1_1_along_z/ppermute | solution.py:350
  74.3 2.9 %experts.13 = (bf16[64,2048]{1,0:T(8,128)(2,1)S(1)}, bf16[64,2048]{1,0:T(8,128)(2,1)S(1)}, s32[8,128]{1,0:T(8,128)S(1)}) custom-call(s32[8,128]{1,0:T(8,128)S(1)} %get-tuple-element.280._, s32[2]{0:T(128)S(1)} %pad_add_fusion.chip_ref, bf16[64,2176]{1,0:T(8,128)(2,1)S(1)} %collective-permute-done.12.refs_0_, ...), custom_call_target="tpu_custom_call" | custom-call | flops 1 | bytes 1 | tf_op jit(solution)/shard_map/experts/pallas_call | solution.py:293
  80.6 2.9 %experts.14 = (bf16[64,2048]{1,0:T(8,128)(2,1)S(1)}, bf16[64,2048]{1,0:T(8,128)(2,1)S(1)}, s32[8,128]{1,0:T(8,128)S(1)}) custom-call(s32[8,128]{1,0:T(8,128)S(1)} %get-tuple-element.294._, s32[2]{0:T(128)S(1)} %pad_add_fusion.chip_ref, bf16[64,2176]{1,0:T(8,128)(2,1)S(1)} %copy-done.4, bf16[64,2176]{1,0:T(8,128)(2,1)S(1)} %collective-permute-done.1.refs_1_, ...), custom_call_target="tpu_custom_call" | custom-call | flops 1 | bytes 1 | tf_op jit(solution)/shard_map/experts/pallas_call | solution.py:293
  83.5 1.9 %collective-permute-done.26 = bf16[64,2048]{1,0:T(8,128)(2,1)S(1)} collective-permute-done((bf16[64,2048]{1,0:T(8,128)(2,1)S(1)}, bf16[64,2048]{1,0:T(8,128)(2,1)S(1)}, u32[]{:S(2)}, u32[]{:S(2)}) %collective-permute-start.26) | collective-permute-done | bytes 262176 | tf_op jit(solution)/shard_map/c2_0_along_z/ppermute | solution.py:350
  85.4 1.9 %collective-permute-done.25 = bf16[64,2048]{1,0:T(8,128)(2,1)S(1)} collective-permute-done((bf16[64,2048]{1,0:T(8,128)(2,1)S(1)}, bf16[64,2048]{1,0:T(8,128)(2,1)S(1)}, u32[]{:S(2)}, u32[]{:S(2)}) %collective-permute-start.25) | collective-permute-done | bytes 262176 | tf_op jit(solution)/shard_map/r3_0_along_y/ppermute | solution.py:354
  91.2 3.4 %experts.15 = (bf16[64,2048]{1,0:T(8,128)(2,1)S(1)}, bf16[64,2048]{1,0:T(8,128)(2,1)S(1)}, s32[8,128]{1,0:T(8,128)}) custom-call(s32[8,128]{1,0:T(8,128)S(1)} %get-tuple-element.316._, s32[2]{0:T(128)S(1)} %pad_add_fusion.chip_ref, bf16[64,2176]{1,0:T(8,128)(2,1)S(1)} %copy-done.3, bf16[64,2176]{1,0:T(8,128)(2,1)S(1)} %collective-permute-done.9.refs_1_, ...), custom_call_target="tpu_custom_call" | custom-call | flops 1 | bytes 1 | tf_op jit(solution)/shard_map/experts/pallas_call | solution.py:293
  97.8 3.3 %collective-permute-done.27 = bf16[64,2048]{1,0:T(8,128)(2,1)S(1)} collective-permute-done((bf16[64,2048]{1,0:T(8,128)(2,1)S(1)}, bf16[64,2048]{1,0:T(8,128)(2,1)S(1)}, u32[]{:S(2)}, u32[]{:S(2)}) %collective-permute-start.27) | collective-permute-done | bytes 262176 | tf_op jit(solution)/shard_map/c3_0_along_z/ppermute | solution.py:350
  101.6 3.6 %collective-permute-done.31 = bf16[64,2048]{1,0:T(8,128)(2,1)S(1)} collective-permute-done((bf16[64,2048]{1,0:T(8,128)(2,1)S(1)}, bf16[64,2048]{1,0:T(8,128)(2,1)S(1)}, u32[]{:S(2)}, u32[]{:S(2)}) %collective-permute-start.31) | collective-permute-done | bytes 262176 | tf_op jit(solution)/shard_map/c3_1_along_z/ppermute | solution.py:350
  (83 shorter events, 35.7 us)
Async XLA Ops:
  0.0 15.1 %collective-permute-start.3 = (bf16[1,512,2048]{2,1,0:T(8,128)(2,1)}, bf16[1,512,2048]{2,1,0:T(8,128)(2,1)}, u32[]{:S(2)}, u32[]{:S(2)}) collective-permute-start(bf16[1,512,2048]{2,1,0:T(8,128)(2,1)} %refs_4_.1), channel_id=1, source_target_pairs={{0,1},{1,0},{2,3},{3,2},{4,5},{5,4},{6,7},{7,6},{8,9},{9,8},{10,11... | collective-permute-start | bytes 6291464 | tf_op jit(solution)/shard_map/ppermute | solution.py:403
  0.5 20.2 %collective-permute-start.6 = (bf16[1,2048,512]{2,1,0:T(8,128)(2,1)}, bf16[1,2048,512]{2,1,0:T(8,128)(2,1)}, u32[]{:S(2)}, u32[]{:S(2)}) collective-permute-start(bf16[1,2048,512]{2,1,0:T(8,128)(2,1)} %refs_3_.1), channel_id=1, source_target_pairs={{0,1},{1,0},{2,3},{3,2},{4,5},{5,4},{6,7},{7,6},{8,9},{9,8},{10,11... | collective-permute-start | bytes 6291464 | tf_op jit(solution)/shard_map/ppermute | solution.py:403
  0.5 20.7 %collective-permute-start.5 = (bf16[1,2048,512]{2,1,0:T(8,128)(2,1)}, bf16[1,2048,512]{2,1,0:T(8,128)(2,1)}, u32[]{:S(2)}, u32[]{:S(2)}) collective-permute-start(bf16[1,2048,512]{2,1,0:T(8,128)(2,1)} %refs_2_.1), channel_id=1, source_target_pairs={{0,1},{1,0},{2,3},{3,2},{4,5},{5,4},{6,7},{7,6},{8,9},{9,8},{10,11... | collective-permute-start | bytes 6291464 | tf_op jit(solution)/shard_map/ppermute | solution.py:403
  6.2 11.7 %collective-permute-start.2 = (bf16[64,2176]{1,0:T(8,128)(2,1)}, bf16[64,2176]{1,0:T(8,128)(2,1)S(1)}, u32[]{:S(2)}, u32[]{:S(2)}) collective-permute-start(bf16[64,2176]{1,0:T(8,128)(2,1)} %get-tuple-element.180.refs_0_), channel_id=1, source_target_pairs={{0,4},{1,5},{2,6},{3,7},{4,8},{5,9},{6,10},{7,11},{8,12},{9,13},{1... | collective-permute-start | bytes 835592 | tf_op jit(solution)/shard_map/z1_0_along_z/ppermute | solution.py:350
  8.5 11.2 %collective-permute-start.1 = (bf16[64,2176]{1,0:T(8,128)(2,1)}, bf16[64,2176]{1,0:T(8,128)(2,1)S(1)}, u32[]{:S(2)}, u32[]{:S(2)}) collective-permute-start(bf16[64,2176]{1,0:T(8,128)(2,1)} %get-tuple-element.180.refs_0_), channel_id=1, source_target_pairs={{0,2},{1,3},{2,0},{3,1},{4,6},{5,7},{6,4},{7,5},{8,10},{9,11},{10,... | collective-permute-start | bytes 835592 | tf_op jit(solution)/shard_map/y0_0_along_y/ppermute | solution.py:354
  17.8 12.1 %collective-permute-start = (bf16[64,2176]{1,0:T(8,128)(2,1)}, bf16[64,2176]{1,0:T(8,128)(2,1)S(1)}, u32[]{:S(2)}, u32[]{:S(2)}) collective-permute-start(bf16[64,2176]{1,0:T(8,128)(2,1)} %get-tuple-element.199.refs_0_), channel_id=1, source_target_pairs={{0,4},{1,5},{2,6},{3,7},{4,8},{5,9},{6,10},{7,11},{8,12},{9,13},{1... | collective-permute-start | bytes 835592 | tf_op jit(solution)/shard_map/z1_1_along_z/ppermute | solution.py:350
  17.9 15.2 %collective-permute-start.9 = (bf16[64,2176]{1,0:T(8,128)(2,1)}, bf16[64,2176]{1,0:T(8,128)(2,1)S(1)}, u32[]{:S(2)}, u32[]{:S(2)}) collective-permute-start(bf16[64,2176]{1,0:T(8,128)(2,1)} %get-tuple-element.199.refs_0_), channel_id=1, source_target_pairs={{0,2},{1,3},{2,0},{3,1},{4,6},{5,7},{6,4},{7,5},{8,10},{9,11},{10,... | collective-permute-start | bytes 835592 | tf_op jit(solution)/shard_map/y0_1_along_y/ppermute | solution.py:354
  19.8 15.1 %collective-permute-start.8 = (bf16[64,2176]{1,0:T(8,128)(2,1)S(1)}, bf16[64,2176]{1,0:T(8,128)(2,1)S(1)}, u32[]{:S(2)}, u32[]{:S(2)}) collective-permute-start(bf16[64,2176]{1,0:T(8,128)(2,1)S(1)} %collective-permute-done.2.refs_0_), channel_id=1, source_target_pairs={{0,4},{1,5},{2,6},{3,7},{4,8},{5,9},{6,10},{7,11},{8,12},{9,13},{1... | collective-permute-start | bytes 835592 | tf_op jit(solution)/shard_map/z2_0_along_z/ppermute | solution.py:350
  20.7 14.2 %collective-permute-start.10 = (bf16[64,2176]{1,0:T(8,128)(2,1)S(1)}, bf16[64,2176]{1,0:T(8,128)(2,1)}, u32[]{:S(2)}, u32[]{:S(2)}) collective-permute-start(bf16[64,2176]{1,0:T(8,128)(2,1)S(1)} %collective-permute-done.2.refs_0_), channel_id=1, source_target_pairs={{0,2},{1,3},{2,0},{3,1},{4,6},{5,7},{6,4},{7,5},{8,10},{9,11},{10,... | collective-permute-start | bytes 835592 | tf_op jit(solution)/shard_map/y1_0_along_y/ppermute | solution.py:354
  29.9 11.4 %collective-permute-start.7 = (bf16[64,2176]{1,0:T(8,128)(2,1)S(1)}, bf16[64,2176]{1,0:T(8,128)(2,1)S(1)}, u32[]{:S(2)}, u32[]{:S(2)}) collective-permute-start(bf16[64,2176]{1,0:T(8,128)(2,1)S(1)} %collective-permute-done.refs_0_), channel_id=1, source_target_pairs={{0,4},{1,5},{2,6},{3,7},{4,8},{5,9},{6,10},{7,11},{8,12},{9,13},{1... | collective-permute-start | bytes 835592 | tf_op jit(solution)/shard_map/z2_1_along_z/ppermute | solution.py:350
  31.6 9.8 %collective-permute-start.15 = (bf16[64,2176]{1,0:T(8,128)(2,1)S(1)}, bf16[64,2176]{1,0:T(8,128)(2,1)S(1)}, u32[]{:S(2)}, u32[]{:S(2)}) collective-permute-start(bf16[64,2176]{1,0:T(8,128)(2,1)S(1)} %collective-permute-done.refs_0_), channel_id=1, source_target_pairs={{0,2},{1,3},{2,0},{3,1},{4,6},{5,7},{6,4},{7,5},{8,10},{9,11},{10,... | collective-permute-start | bytes 835592 | tf_op jit(solution)/shard_map/y1_1_along_y/ppermute | solution.py:354
  34.8 13.0 %collective-permute-start.14 = (bf16[64,2176]{1,0:T(8,128)(2,1)S(1)}, bf16[64,2176]{1,0:T(8,128)(2,1)S(1)}, u32[]{:S(2)}, u32[]{:S(2)}) collective-permute-start(bf16[64,2176]{1,0:T(8,128)(2,1)S(1)} %collective-permute-done.8.refs_0_), channel_id=1, source_target_pairs={{0,4},{1,5},{2,6},{3,7},{4,8},{5,9},{6,10},{7,11},{8,12},{9,13},{1... | collective-permute-start | bytes 835592 | tf_op jit(solution)/shard_map/z3_0_along_z/ppermute | solution.py:350
  35.4 12.7 %collective-permute-start.16 = (bf16[64,2176]{1,0:T(8,128)(2,1)S(1)}, bf16[64,2176]{1,0:T(8,128)(2,1)S(1)}, u32[]{:S(2)}, u32[]{:S(2)}) collective-permute-start(bf16[64,2176]{1,0:T(8,128)(2,1)S(1)} %collective-permute-done.8.refs_0_), channel_id=1, source_target_pairs={{0,2},{1,3},{2,0},{3,1},{4,6},{5,7},{6,4},{7,5},{8,10},{9,11},{10,... | collective-permute-start | bytes 835592 | tf_op jit(solution)/shard_map/y2_0_along_y/ppermute | solution.py:354
  40.0 12.8 %collective-permute-start.13 = (bf16[64,2048]{1,0:T(8,128)(2,1)S(1)}, bf16[64,2048]{1,0:T(8,128)(2,1)S(1)}, u32[]{:S(2)}, u32[]{:S(2)}) collective-permute-start(bf16[64,2048]{1,0:T(8,128)(2,1)S(1)} %get-tuple-element.222), channel_id=1, source_target_pairs={{0,2},{1,3},{2,0},{3,1},{4,6},{5,7},{6,4},{7,5},{8,10},{9,11},{10,... | collective-permute-start | bytes 786440 | tf_op jit(solution)/shard_map/r1_0_along_y/ppermute | solution.py:354
  44.2 10.8 %collective-permute-start.12 = (bf16[64,2176]{1,0:T(8,128)(2,1)S(1)}, bf16[64,2176]{1,0:T(8,128)(2,1)S(1)}, u32[]{:S(2)}, u32[]{:S(2)}) collective-permute-start(bf16[64,2176]{1,0:T(8,128)(2,1)S(1)} %collective-permute-done.7.refs_0_), channel_id=1, source_target_pairs={{0,4},{1,5},{2,6},{3,7},{4,8},{5,9},{6,10},{7,11},{8,12},{9,13},{1... | collective-permute-start | bytes 835592 | tf_op jit(solution)/shard_map/z3_1_along_z/ppermute | solution.py:350
  46.1 12.6 %collective-permute-start.11 = (bf16[64,2176]{1,0:T(8,128)(2,1)S(1)}, bf16[64,2176]{1,0:T(8,128)(2,1)S(1)}, u32[]{:S(2)}, u32[]{:S(2)}) collective-permute-start(bf16[64,2176]{1,0:T(8,128)(2,1)S(1)} %collective-permute-done.7.refs_0_), channel_id=1, source_target_pairs={{0,2},{1,3},{2,0},{3,1},{4,6},{5,7},{6,4},{7,5},{8,10},{9,11},{10,... | collective-permute-start | bytes 835592 | tf_op jit(solution)/shard_map/y2_1_along_y/ppermute | solution.py:354
  47.9 13.8 %collective-permute-start.17 = (bf16[64,2048]{1,0:T(8,128)(2,1)S(1)}, bf16[64,2048]{1,0:T(8,128)(2,1)S(1)}, u32[]{:S(2)}, u32[]{:S(2)}) collective-permute-start(bf16[64,2048]{1,0:T(8,128)(2,1)S(1)} %get-tuple-element.253), channel_id=1, source_target_pairs={{0,4},{1,5},{2,6},{3,7},{4,8},{5,9},{6,10},{7,11},{8,12},{9,13},{1... | collective-permute-start | bytes 786440 | tf_op jit(solution)/shard_map/r1_1_along_z/ppermute | solution.py:350
  52.7 11.9 %collective-permute-start.18 = (bf16[64,2176]{1,0:T(8,128)(2,1)S(1)}, bf16[64,2176]{1,0:T(8,128)(2,1)S(1)}, u32[]{:S(2)}, u32[]{:S(2)}) collective-permute-start(bf16[64,2176]{1,0:T(8,128)(2,1)S(1)} %collective-permute-done.14.refs_0_), channel_id=1, source_target_pairs={{0,2},{1,3},{2,0},{3,1},{4,6},{5,7},{6,4},{7,5},{8,10},{9,11},{10,... | collective-permute-start | bytes 835592 | tf_op jit(solution)/shard_map/y3_0_along_y/ppermute | solution.py:354
  54.3 13.5 %collective-permute-start.19 = (bf16[64,2048]{1,0:T(8,128)(2,1)S(1)}, bf16[64,2048]{1,0:T(8,128)(2,1)S(1)}, u32[]{:S(2)}, u32[]{:S(2)}) collective-permute-start(bf16[64,2048]{1,0:T(8,128)(2,1)S(1)} %get-tuple-element.261), channel_id=1, source_target_pairs={{0,2},{1,3},{2,0},{3,1},{4,6},{5,7},{6,4},{7,5},{8,10},{9,11},{10,... | collective-permute-start | bytes 786440 | tf_op jit(solution)/shard_map/r2_0_along_y/ppermute | solution.py:354
  63.8 10.5 %collective-permute-start.23 = (bf16[64,2176]{1,0:T(8,128)(2,1)S(1)}, bf16[64,2176]{1,0:T(8,128)(2,1)S(1)}, u32[]{:S(2)}, u32[]{:S(2)}) collective-permute-start(bf16[64,2176]{1,0:T(8,128)(2,1)S(1)} %collective-permute-done.11.refs_1_), channel_id=1, source_target_pairs={{0,4},{1,5},{2,6},{3,7},{4,8},{5,9},{6,10},{7,11},{8,12},{9,13},{1... | collective-permute-start | bytes 835592 | tf_op jit(solution)/shard_map/y3_1_along_z/ppermute | solution.py:350
  78.6 17.1 %collective-permute-start.29 = (bf16[64,2048]{1,0:T(8,128)(2,1)S(1)}, bf16[64,2048]{1,0:T(8,128)(2,1)S(1)}, u32[]{:S(2)}, u32[]{:S(2)}) collective-permute-start(bf16[64,2048]{1,0:T(8,128)(2,1)S(1)} %get-tuple-element.321), channel_id=1, source_target_pairs={{0,2},{1,3},{2,0},{3,1},{4,6},{5,7},{6,4},{7,5},{8,10},{9,11},{10,... | collective-permute-start | bytes 786440 | tf_op jit(solution)/shard_map/r3_1_along_y/ppermute | solution.py:354
  87.4 9.5 %collective-permute-start.30 = (bf16[64,2048]{1,0:T(8,128)(2,1)S(1)}, bf16[64,2048]{1,0:T(8,128)(2,1)S(1)}, u32[]{:S(2)}, u32[]{:S(2)}) collective-permute-start(bf16[64,2048]{1,0:T(8,128)(2,1)S(1)} %add_convert_fusion.4), channel_id=1, source_target_pairs={{0,4},{1,5},{2,6},{3,7},{4,8},{5,9},{6,10},{7,11},{8,12},{9,13},{1... | collective-permute-start | bytes 786440 | tf_op jit(solution)/shard_map/c2_1_along_z/ppermute | solution.py:350
  89.0 12.2 %collective-permute-start.27 = (bf16[64,2048]{1,0:T(8,128)(2,1)S(1)}, bf16[64,2048]{1,0:T(8,128)(2,1)S(1)}, u32[]{:S(2)}, u32[]{:S(2)}) collective-permute-start(bf16[64,2048]{1,0:T(8,128)(2,1)S(1)} %add_convert_fusion.3), channel_id=1, source_target_pairs={{0,4},{1,5},{2,6},{3,7},{4,8},{5,9},{6,10},{7,11},{8,12},{9,13},{1... | collective-permute-start | bytes 786440 | tf_op jit(solution)/shard_map/c3_0_along_z/ppermute | solution.py:350
  90.2 10.9 %collective-permute-start.24 = (bf16[64,2048]{1,0:T(8,128)(2,1)S(1)}, bf16[64,2048]{1,0:T(8,128)(2,1)S(1)}, u32[]{:S(2)}, u32[]{:S(2)}) collective-permute-start(bf16[64,2048]{1,0:T(8,128)(2,1)S(1)} %get-tuple-element.297), channel_id=1, source_target_pairs={{0,2},{1,3},{2,0},{3,1},{4,6},{5,7},{6,4},{7,5},{8,10},{9,11},{10,... | collective-permute-start | bytes 786440 | tf_op jit(solution)/shard_map/r0_0_along_y/ppermute | solution.py:354
  (19 other events, 150.8 us)
